TPU v7x, 128 devices: a whole 4x4x4 slice. The times are simulated.
128 devices in a mesh: ens: 4 (over x), sp: 32 (over y, z, core).
Axes of the slice: x: 4, y: 4, z: 4, core: 2. Of those that a mesh axis runs over, the one named last changes fastest.
Arguments:
- latent: bfloat16 [8, 32768, 1024], P('ens', 'sp'), may hold values from -6 to 6
- w_in: bfloat16 [1024, 1024], replicated, may hold values from -0.1875 to 0.1875
- output_weight: bfloat16 [80, 1024], replicated, may hold values from -0.1875 to 0.1875
- targets: bfloat16 [80, 32768], P(None, 'sp'), may hold values from -6 to 6
- area_weights: float32 [32768], P('sp'), may hold values from 1 to 300, as said below
- live_counts: int32 [32], P('sp'), may hold values from 1 to 1024, 28672 in all
Outputs:
- loss: float32 [], replicated
- grad_latent: bfloat16 [8, 32768, 1024], P('ens', 'sp')
- grad_w_in: float32 [1024, 1024], P('sp')
- grad_w_out: float32 [80, 1024], replicated
Inputs may be any that keep to these rules, and one draw needn't show every extreme that they name: `area_weights`: weights of one block of 1024 points share a factor that differs between blocks. `live_counts`: each entry counts the owned points at the start of one block of 1024; some entry equals 1024.
All inputs are finite; a program needn't handle non-finite values.
Results may differ from a plain program's by a relative error of at most 0.0095.
Values may be sent and summed in bfloat16 or wider, within the bound.
A program may use at most 128 MiB of HBM per device.

v0:
```python
import jax
import jax.numpy as jnp
from jax import lax
from jax.sharding import PartitionSpec as P

loss_scale = 1024.0
smoothing = 1.0


def partial_skill_terms(members, measured_target_slice, kernel_softening_widths):
    n_members = members.shape[0]
    diff_obs = members - measured_target_slice[None]
    obs_norm = jnp.sqrt(jnp.sum(diff_obs * diff_obs, axis=1) + smoothing)
    pair_diff = members[:, None] - members[None, :]
    pair_norm = jnp.sqrt(jnp.sum(pair_diff * pair_diff, axis=2) + smoothing)
    spread = jnp.sum(pair_norm, axis=(0, 1)) - n_members * 1.0
    ensemble_skill_values = jnp.sum(obs_norm, axis=0) / n_members - spread / (
        2.0 * n_members * (n_members - 1)
    )
    derivative_coefficients = diff_obs / (n_members * obs_norm[:, None]) - jnp.sum(
        pair_diff / pair_norm[:, :, None], axis=1
    ) / (n_members * (n_members - 1))
    return (ensemble_skill_values, derivative_coefficients * kernel_softening_widths[None, None])


def per_device(latent, w_in, output_weight, targets, area_weights, live_counts):
    mem_dev, points, feature_width = latent.shape
    groups = lax.axis_size("ens")
    ens_index = lax.axis_index("ens")
    position = jnp.arange(points, dtype=jnp.int32)
    is_live = (position < live_counts[0]).astype(jnp.float32)
    weighted = area_weights * is_live
    weight_total, live_total = lax.psum((jnp.sum(weighted), jnp.sum(is_live)), "sp")
    scales_all = loss_scale * live_total * weighted / weight_total
    pre_act = jnp.einsum("mph,hk->mpk", latent, w_in, preferred_element_type=jnp.float32)
    latent_activations = jax.nn.gelu(pre_act).astype(jnp.bfloat16)
    ensemble_prediction = jnp.einsum(
        "mp,hjp->hmj", output_weight, latent_activations, preferred_element_type=jnp.float32
    ).astype(jnp.bfloat16)
    block_len = points // groups
    offset = ens_index * block_len
    members_regathered = lax.all_to_all(
        ensemble_prediction, "ens", split_axis=2, concat_axis=0, tiled=True
    )
    measured_target_slice = lax.dynamic_slice_in_dim(targets, offset, block_len, 1).astype(
        jnp.float32
    )
    kernel_softening_widths = lax.dynamic_slice_in_dim(scales_all, offset, block_len, 0)
    weight_block = lax.dynamic_slice_in_dim(weighted, offset, block_len, 0)
    ensemble_skill_values, derivative_coefficients = partial_skill_terms(
        members_regathered.astype(jnp.float32), measured_target_slice, kernel_softening_widths
    )
    loss_sum = lax.psum(jnp.sum(weight_block * ensemble_skill_values), ("ens", "sp"))
    slopes_own = lax.all_to_all(
        derivative_coefficients.astype(jnp.bfloat16), "ens", split_axis=0, concat_axis=2, tiled=True
    )
    back_hidden = jnp.einsum(
        "vk,mvp->mpk", output_weight, slopes_own, preferred_element_type=jnp.float32
    )
    unused_out, gelu_pull = jax.vjp(jax.nn.gelu, pre_act)
    back_pre = gelu_pull(back_hidden)[0].astype(jnp.bfloat16)
    grad_latent = jnp.einsum(
        "mpk,hk->mph", back_pre, w_in, preferred_element_type=jnp.float32
    ).astype(jnp.bfloat16)
    head_term = jnp.einsum(
        "mvp,mpk->vk", slopes_own, latent_activations, preferred_element_type=jnp.float32
    )
    row_share = feature_width // lax.axis_size("sp")
    input_term = jnp.einsum("mph,mpk->hk", latent, back_pre, preferred_element_type=jnp.float32)
    input_sum, output_sum = lax.psum((input_term, head_term), ("ens", "sp"))
    row_offset = lax.axis_index("sp") * row_share
    input_rows = lax.dynamic_slice_in_dim(input_sum, row_offset, row_share, 0)
    return (loss_sum / weight_total, grad_latent, input_rows / live_total, output_sum / live_total)


def solution(mesh):
    placed = (P("ens", "sp", None), P(), P(), P(None, "sp"), P("sp"), P("sp"))
    return jax.shard_map(
        per_device,
        mesh=mesh,
        in_specs=placed,
        out_specs=(P(), P("ens", "sp", None), P("sp", None), P()),
        check_vma=False,
    )
```

profile of v0, /device:TPU:1, one launch (start us, length us, event | category | flops | bytes accessed | tf_op | source)
XLA Modules:
  0.0 296.2 jit_solution(7909548073176238129)
XLA Ops:
  7.2 0.0 copy-start
  7.2 0.0 copy-start.3
  7.2 1.6 copy-done
  8.8 10.8 %multiply_convert_fusion = (bf16[2,1024,1024]{2,1,0:T(8,128)(2,1)S(1)}, f32[2,1024,1024]{2,1,0:T(8,128)}) fusion(bf16[2,1024,1024]{2,1,0:T(8,128)(2,1)} %param.6, bf16[1024,1024]{1,0:T(8,128)(2,1)S(1)} %copy-done), kind=kOutput, calls=%fused_computation.9 | convolution fusion | flops 4313841664 | bytes 18874368 | tf_op jit(solution)/shard_map/mph,hk->mpk/dot_general | solution.py:35
  19.6 0.0 copy-start.1
  19.6 0.0 copy-start.4
  19.6 2.0 copy-done.1
  21.6 0.0 copy-done.3
  21.6 1.4 fusion.12
  23.0 1.1 copy.36
  24.1 4.8 %all-to-all-start = ((bf16[2,80,1024]{1,0,2:T(2,128)(2,1)}), bf16[2,80,1024]{1,0,2:T(2,128)(2,1)S(1)}, u32[]{:S(2)}, u32[]{:S(2)}) async-start(bf16[2,80,1024]{1,0,2:T(2,128)(2,1)} %copy.36), calls=%async_computation | async-start | bytes 1048576 | tf_op jit(solution)/shard_map/all_to_all | solution.py:42
  28.9 0.0 all-reduce.4.cloned.1.call-start
  29.6 0.0 copy-done.4
  29.6 0.6 fusion.18
  30.2 65.2 %all-reduce.1 = (f32[]{:T(128)}, f32[]{:T(128)}) all-reduce(f32[]{:T(128)} %get-tuple-element.32, f32[]{:T(128)} %get-tuple-element.40), channel_id=1, replica_groups=mesh['ens'=4,'sp'=32] {'sp'}, use_global_device_ids=true, to_apply=%region_7.0 | all-reduce | flops 2 | bytes 16 | tf_op jit(solution)/shard_map/psum | solution.py:33
  96.1 0.7 multiply_divide_fusion
  96.8 0.1 dynamic_slice.14
  96.9 0.8 dynamic-slice_convert_fusion
  97.7 0.0 all-to-all-done
  97.7 0.4 copy.37
  98.1 0.3 reshape.46
  98.4 0.2 multiply_reduce_fusion
  98.6 0.0 copy-start.2
  98.6 0.1 copy.38
  98.8 0.7 fusion.8
  99.5 0.0 copy-start.6
  99.5 0.6 fusion.7
  100.1 0.2 multiply_convert_fusion.1
  100.3 10.5 %all_to_all.27 = bf16[8,80,256]{2,1,0:T(8,128)(2,1)S(1)} all-to-all(bf16[8,80,256]{2,1,0:T(8,128)(2,1)S(1)} %multiply_convert_fusion.1), channel_id=1, replica_groups=mesh['ens'=4,'sp'=32] {'ens'}, dimensions={0} | all-to-all | bytes 655360 | tf_op jit(solution)/shard_map/all_to_all | solution.py:54
  110.8 0.0 copy-done.2
  110.8 1.6 convolution_bitcast_fusion.1
  112.4 0.0 copy-done.6
  112.4 0.0 copy-start.5
  112.4 7.3 %fusion.6 = bf16[2,1024,1024]{2,1,0:T(8,128)(2,1)} fusion(f32[2,1024,1024]{2,1,0:T(8,128)S(1)} %copy-done.6, bf16[2,80,1024]{2,1,0:T(8,128)(2,1)S(1)} %bitcast.44, bf16[80,1024]{1,0:T(8,128)(2,1)S(1)} %copy-done.3), kind=kOutput, calls=%fused_computation.8 | convolution fusion | flops 377487360 | bytes 13074432 | tf_op jit(solution)/shard_map/vk,mvp->mpk/dot_general | solution.py:57
  119.7 0.0 copy-done.5
  119.7 8.3 %convolution_bitcast_fusion = f32[1024,1024]{0,1:T(8,128)} fusion(bf16[2,1024,1024]{2,1,0:T(8,128)(2,1)} %fusion.6, bf16[2,1024,1024]{2,1,0:T(8,128)(2,1)S(1)} %copy-done.5), kind=kOutput, calls=%fused_computation.15 | convolution fusion | flops 4294967296 | bytes 12582912 | tf_op jit(solution)/shard_map/mph,mpk->hk/dot_general | solution.py:69
  128.0 0.0 all-reduce.4.cloned.1.call-update
  128.0 0.7 multiply_reduce_fusion.1
  128.7 68.5 %psum.35 = f32[]{:T(128)} all-reduce(f32[]{:T(128)} %multiply_reduce_fusion.1), channel_id=1, replica_groups=mesh['ens'=4,'sp'=32] {'ens','sp'}, use_global_device_ids=true, to_apply=%region_5.0 | all-reduce | flops 1 | bytes 8 | tf_op jit(solution)/shard_map/psum | solution.py:53
  198.5 8.3 %convolution_convert_fusion = bf16[2,1024,1024]{2,1,0:T(8,128)(2,1)} fusion(bf16[2,1024,1024]{2,1,0:T(8,128)(2,1)} %fusion.6, bf16[1024,1024]{1,0:T(8,128)(2,1)S(1)} %copy-done), kind=kOutput, calls=%fused_computation.14 | convolution fusion | flops 4297064448 | bytes 10485760 | tf_op jit(solution)/shard_map/mpk,hk->mph/dot_general | solution.py:62
  206.9 76.2 %all-reduce.4.cloned.1.call-done = (f32[1024,1024]{0,1:T(8,128)}, f32[80,1024]{1,0:T(8,128)}) async-done(((f32[1024,1024]{0,1:T(8,128)}, f32[80,1024]{1,0:T(8,128)}), (f32[1024,1024]{0,1:T(8,128)}, f32[80,1024]{1,0:T(8,128)})) %all-reduce.4.cloned.1.call-update) | async-done | bytes 4522000 | tf_op jit(solution)/shard_map/psum | solution.py:70
  283.0 1.9 dynamic-slice_divide_fusion
  285.0 0.8 copy.42
  285.8 2.4 broadcast_divide_fusion
  (5 shorter events, 0.1 us)
Async XLA Ops:
  7.2 1.6 copy-start
  7.2 14.4 %copy-start.3 = (bf16[80,1024]{1,0:T(8,128)(2,1)S(1)}, bf16[80,1024]{1,0:T(8,128)(2,1)}, u32[]{:S(2)}) copy-start(bf16[80,1024]{1,0:T(8,128)(2,1)} %param.8) | copy-start | bytes 491524
  19.6 2.0 copy-start.1
  19.6 10.0 %copy-start.4 = (f32[1024]{0:T(1024)S(1)}, f32[1024]{0:T(1024)}, u32[]{:S(2)}) copy-start(f32[1024]{0:T(1024)} %param.10) | copy-start | bytes 12292
  24.1 73.6 %all-to-all-start = ((bf16[2,80,1024]{1,0,2:T(2,128)(2,1)}), bf16[2,80,1024]{1,0,2:T(2,128)(2,1)S(1)}, u32[]{:S(2)}, u32[]{:S(2)}) async-start(bf16[2,80,1024]{1,0,2:T(2,128)(2,1)} %copy.36), calls=%async_computation | async-start | bytes 1048576 | tf_op jit(solution)/shard_map/all_to_all | solution.py:42
  28.9 254.1 %all-reduce.4.cloned.1.call-start = ((), (), s32[]{:S(2)}) async-start(), calls=%async_computation.2 | async-start | bytes 9043968 | tf_op jit(solution)/shard_map/psum | solution.py:70
  98.6 12.2 %copy-start.2 = (bf16[2,1024,1024]{2,1,0:T(8,128)(2,1)S(1)}, bf16[2,1024,1024]{2,1,0:T(8,128)(2,1)}, u32[]{:S(2)}) copy-start(bf16[2,1024,1024]{2,1,0:T(8,128)(2,1)} %copy-done.1) | copy-start | bytes 12582916
  99.5 12.9 %copy-start.6 = (f32[2,1024,1024]{2,1,0:T(8,128)S(1)}, f32[2,1024,1024]{2,1,0:T(8,128)}, u32[]{:S(2)}) copy-start(f32[2,1024,1024]{2,1,0:T(8,128)} %get-tuple-element.39) | copy-start | bytes 25165828
  112.4 7.3 %copy-start.5 = (bf16[2,1024,1024]{2,1,0:T(8,128)(2,1)S(1)}, bf16[2,1024,1024]{2,1,0:T(8,128)(2,1)}, u32[]{:S(2)}) copy-start(bf16[2,1024,1024]{2,1,0:T(8,128)(2,1)} %param.6) | copy-start | bytes 12582916
Sparse Core Ops, SparseCore 0:
  128.2 154.8 all-reduce.3
where the time goes:
time: 297 us; the launch traced here: 296 us
  blocking collectives  144 us (48%)
  waiting for transfers between devices  76.2 us (26%)
  matrix products  37.7 us (13%)
  between operations  18 us (6%)
  other arithmetic  8.8 us (3%)
  local copies, waits for them, and re-layouts  6.48 us (2%)
  starting transfers between devices  4.84 us (2%)
    psum x1, waiting for transfers between devices, per_device(): input_sum, output_sum = lax.psum((input_term, head_term), ('ens', 'sp'))  76.2 us
    psum x1, blocking collectives, per_device(): lax.psum(jnp.sum(weight_block * ensemble_skill_values), ('ens', 'sp'))  68.5 us
    psum x1, blocking collectives, per_device(): lax.psum((jnp.sum(weighted), jnp.sum(is_live)), 'sp')  65.2 us
    dot_general x1, matrix products, per_device(): jnp.einsum('mph,hk->mpk', latent, w_in, preferred_element_type=jnp.float32)  10.8 us
    all_to_all x1, blocking collectives, per_device(): lax.all_to_all(derivative_coefficients.astype(jnp.bfloat16), 'ens', split...  10.5 us
    dot_general x1, matrix products, per_device(): jnp.einsum('mpk,hk->mph', back_pre, w_in, preferred_element_type=jnp.floa...  8.31 us
    dot_general x1, matrix products, per_device(): jnp.einsum('mph,mpk->hk', latent, back_pre, preferred_element_type=jnp.fl...  8.3 us
    dot_general x1, matrix products, per_device(): jnp.einsum('vk,mvp->mpk', output_weight, slopes_own, preferred_element_ty...  7.31 us
  transfers between devices with their start and end apart: 2, of which 1 were waited for; matrix products, arithmetic and copies ran while one was open for 4% of the time, Pallas kernels for 0%

commit v1 on v0

v1 whole, which is shorter than its diff:
```python
import functools
import math

import jax
import jax.numpy as jnp
from jax import lax
from jax.experimental import pallas as pl
from jax.experimental.pallas import tpu as pltpu
from jax.sharding import PartitionSpec as P

BF16, F32 = jnp.bfloat16, jnp.float32
MESH = pl.DeviceIdType.MESH
LOSS_SCALE = 1024.0
MEMBERS, VARS, FEATURES, POINTS = 8, 80, 1024, 1024
CHUNKS = 2
CHUNK = POINTS // CHUNKS
LANES = 128
PIECES = 2
WIDE = FEATURES // PIECES
ROWS = 32
OUTER = math.sqrt(2.0 / math.pi)
INNER = OUTER * 0.044715


def dot(a, b, ca, cb):
    return lax.dot_general(a, b, (((ca,), (cb,)), ((), ())), preferred_element_type=F32)


def activation(z):
    cubic = INNER * (z * z)
    s = 0.5 * jnp.tanh(z * (cubic + OUTER)) + 0.5
    h = z * s
    slope = s + (h - h * s) * (6.0 * cubic + 2.0 * OUTER)
    return h.astype(BF16), slope.astype(BF16)


def score_block(x_ref, y, weighted, scales, store):
    n = MEMBERS
    pairs = [(i, j) for i in range(n) for j in range(i + 1, n)]
    step = 16
    own = [jnp.zeros((step, LANES), F32) for _ in range(n)]
    between = [jnp.zeros((step, LANES), F32) for _ in pairs]
    for v in range(0, VARS, step):
        x = [x_ref[m // 2, m % 2, v : v + step, :].astype(F32) for m in range(n)]
        for m in range(n):
            d = x[m] - y[v : v + step]
            own[m] = own[m] + d * d
        for q, (i, j) in enumerate(pairs):
            d = x[i] - x[j]
            between[q] = between[q] + d * d
    a = [jnp.sqrt(jnp.sum(o, axis=0, keepdims=True) + 1.0) for o in own]
    b = [jnp.sqrt(jnp.sum(o, axis=0, keepdims=True) + 1.0) for o in between]
    score = sum(a) / n - sum(b) / (n * (n - 1.0))
    from_target = [scales / (n * t) for t in a]
    from_pair = [scales / (n * (n - 1.0) * t) for t in b]
    for v in range(0, VARS, step):
        x = [x_ref[m // 2, m % 2, v : v + step, :].astype(F32) for m in range(n)]
        total = [(x[m] - y[v : v + step]) * from_target[m] for m in range(n)]
        for q, (i, j) in enumerate(pairs):
            d = (x[i] - x[j]) * from_pair[q]
            total[i] = total[i] - d
            total[j] = total[j] + d
        for m in range(n):
            store(m, v, step, total[m].astype(BF16))
    return weighted * score


def kernel(
    lat_hbm, w_hbm, wout, targets, area, live,
    loss_out, glat_hbm, gwin_out, gwout_out,
    lat, w, hid, back, acc, fsend, frecv, ssend, srecv, gout, gparts,
    core_send, core_recv, one_send, one_recv, two_send, two_recv, three,
    g_core_send, g_core_recv, g_y_send, g_y_recv, g_z, g_x, g_all,
    wt_core, wt_z, wt_y, ls_core, ls_y, ls_z, ls_x,
    in_sem, out_sem, f_ss, f_rs, s_ss, s_rs, p_ss, p_rs, g_ss, g_rs, t_ss, t_rs,
):
    e = lax.axis_index("ens")
    sp = lax.axis_index("sp")
    core = lax.rem(sp, 2)
    z = lax.rem(sp // 2, 4)
    y = sp // 8

    def turn(i, d):
        return lax.rem(i + d, 4)

    def device(x_, y_, z_, core_):
        return (x_, (y_ * 4 + z_) * 2 + core_)

    along = {
        "x": lambda d: device(turn(e, d), y, z, core),
        "y": lambda d: device(e, turn(y, d), z, core),
        "z": lambda d: device(e, y, turn(z, d), core),
    }
    place = {"x": e, "y": y, "z": z}
    sibling = device(e, y, z, 1 - core)

    def load(m, c):
        s = pl.ds(c * CHUNK, CHUNK)
        return pltpu.make_async_copy(lat_hbm.at[m, s], lat.at[m, s], in_sem.at[1 + 2 * c + m])

    load_w = pltpu.make_async_copy(w_hbm, w, in_sem.at[0])
    load_w.start()
    loads = {(c, m): load(m, c) for c in range(CHUNKS) for m in range(2)}
    for cp in loads.values():
        cp.start()

    peers = [along[k](d) for k in "xyz" for d in (1, 2, 3)] + [sibling]
    peers += [device(e, turn(y, d), z, 1 - core) for d in (1, 2, 3)]
    barrier = pltpu.get_barrier_semaphore()
    for p in peers:
        pl.semaphore_signal(barrier, inc=1, device_id=p, device_id_type=MESH)

    def send(src, dst, ss, rs, to):
        cp = pltpu.make_async_remote_copy(
            src_ref=src, dst_ref=dst, send_sem=ss, recv_sem=rs, device_id=to, device_id_type=MESH
        )
        cp.start()
        return cp

    started = []

    def spread(axis, src, dst, ss, rs):
        cps = []
        for d in (2, 1, 3):
            cps.append(send(src(turn(place[axis], d)), dst(d, place[axis]), ss.at[d - 1], rs.at[d - 1], along[axis](d)))
        started.extend(cps)
        return cps

    def arrive(cps):
        for cp in cps:
            cp.wait_recv()

    where = lax.broadcasted_iota(jnp.int32, (8, LANES), 0) * LANES + lax.broadcasted_iota(jnp.int32, (8, LANES), 1)
    is_live = (where < live[0]).astype(F32)
    weighted_all = area[...] * is_live
    first = lax.broadcasted_iota(jnp.int32, (8, LANES), 0) == 0
    wt_own = jnp.where(
        first, jnp.sum(weighted_all, axis=0, keepdims=True), jnp.sum(is_live, axis=0, keepdims=True)
    )
    wt_core[core] = wt_own

    def forward(c, m):
        loads[c, m].wait()
        s = pl.ds(c * CHUNK, CHUNK)
        pre = jnp.dot(lat[m, s, :], w[...], preferred_element_type=F32)
        h, g = activation(pre)
        hid[m, s, :] = h
        back[m, s, :] = g
        f = dot(wout[...], hid[m, s, :], 1, 1).astype(BF16)
        for k in range(4):
            fsend[c, k, m] = f[:, k * LANES : (k + 1) * LANES]
        frecv[c, e, m] = fsend[c, e, m]

    def forward_send(c, m):
        return spread(
            "x", lambda k: fsend.at[c, k, m], lambda d, own: frecv.at[c, own, m], f_ss.at[c, m], f_rs.at[c, m]
        )

    loss_rows = []

    def scored(c):
        block = c * 4 + e
        y_block = targets[:, pl.ds(pl.multiple_of(block * LANES, LANES), LANES)].astype(F32)
        lanes = lax.broadcasted_iota(jnp.int32, (1, LANES), 1)
        weighted = area[pl.ds(block, 1), :] * (block * LANES + lanes < live[0]).astype(F32)
        scales = LOSS_SCALE * live_total * weighted / weight_total

        def store(m, v, step, value):
            ssend[c, m // 2, m % 2, v : v + step, :] = value

        loss_rows.append(score_block(frecv.at[c], y_block, weighted, scales, store))
        srecv[c, e] = ssend[c, e]
        return spread("x", lambda k: ssend.at[c, k], lambda d, own: srecv.at[c, own], s_ss.at[c], s_rs.at[c])

    load_w.wait()
    forward(0, 0)
    pl.semaphore_wait(barrier, len(peers))
    f00 = forward_send(0, 0)
    tw = send(wt_core.at[core], wt_core.at[core], t_ss.at[0], t_rs.at[0], sibling)
    started.append(tw)
    forward(0, 1)
    f01 = forward_send(0, 1)
    arrive([tw])
    wt_z[z] = wt_core[0] + wt_core[1]
    tw = spread("z", lambda k: wt_z.at[z], lambda d, own: wt_z.at[own], t_ss.at[pl.ds(1, 3)], t_rs.at[pl.ds(1, 3)])
    forward(1, 0)
    f10 = forward_send(1, 0)
    arrive(tw)
    wt_y[y] = (wt_z[0] + wt_z[1]) + (wt_z[2] + wt_z[3])
    tw = spread("y", lambda k: wt_y.at[y], lambda d, own: wt_y.at[own], t_ss.at[pl.ds(4, 3)], t_rs.at[pl.ds(4, 3)])
    forward(1, 1)
    f11 = forward_send(1, 1)
    arrive(tw)
    totals = jnp.sum((wt_y[0] + wt_y[1]) + (wt_y[2] + wt_y[3]), axis=1, keepdims=True)
    weight_total = totals[0:1, 0:1]
    live_total = totals[1:2, 0:1]

    arrive(f00)
    arrive(f01)
    s0 = scored(0)
    arrive(f10)
    arrive(f11)
    s1 = scored(1)

    def backward(c):
        s = pl.ds(c * CHUNK, CHUNK)
        for m in range(2):
            slopes = jnp.concatenate([srecv[c, k, m] for k in range(4)], axis=1)
            bh = dot(slopes, wout[...], 0, 0)
            back[m, s, :] = (back[m, s, :].astype(F32) * bh).astype(BF16)
            part = dot(slopes, hid[m, s, :], 1, 0)
            if c == 0 and m == 0:
                gout[...] = part
            else:
                gout[...] += part

    def weight_piece(c, j):
        s = pl.ds(c * CHUNK, CHUNK)
        cols = slice(j * WIDE, (j + 1) * WIDE)
        a = lat[:, s, :].reshape(2 * CHUNK, FEATURES)
        b = back[:, s, cols].reshape(2 * CHUNK, WIDE)
        return dot(a, b, 0, 0).reshape(2 * 16, ROWS, WIDE)

    arrive(s0)
    backward(0)
    for j in range(PIECES):
        acc[j] = weight_piece(0, j)

    loss_tile = jnp.broadcast_to(loss_rows[0] + loss_rows[1], (8, LANES))
    ls_core[core] = loss_tile
    lc = send(ls_core.at[core], ls_core.at[core], t_ss.at[7], t_rs.at[7], sibling)
    started.append(lc)

    arrive(s1)
    backward(1)

    def g_start():
        def body(k, _):
            cols = pl.ds(pl.multiple_of((k * 2 + 1 - core) * LANES, LANES), LANES)
            g_core_send[k] = gout[:, cols].astype(BF16)
            return 0

        lax.fori_loop(0, 4, body, 0)
        cp = send(g_core_send, g_core_recv, g_ss.at[0], g_rs.at[0], sibling)
        started.append(cp)
        return [cp]

    def g_to_y(cps):
        arrive(cps)

        def body(k, _):
            cols = pl.ds(pl.multiple_of((k * 2 + core) * LANES, LANES), LANES)
            g_y_send[k] = (gout[:, cols] + g_core_recv[k].astype(F32)).astype(BF16)
            return 0

        lax.fori_loop(0, 4, body, 0)
        return spread(
            "y", lambda k: g_y_send.at[k], lambda d, own: g_y_recv.at[d - 1], g_ss.at[pl.ds(1, 3)], g_rs.at[pl.ds(1, 3)]
        )

    def g_to_z(cps):
        arrive(cps)
        total = g_y_send[y].astype(F32)
        for d in range(3):
            total = total + g_y_recv[d].astype(F32)
        g_z[z] = total.astype(BF16)
        return spread(
            "z", lambda k: g_z.at[z], lambda d, own: g_z.at[own], g_ss.at[pl.ds(4, 3)], g_rs.at[pl.ds(4, 3)]
        )

    def four(ref):
        return (ref[0].astype(F32) + ref[1].astype(F32)) + (ref[2].astype(F32) + ref[3].astype(F32))

    def g_to_x(cps):
        arrive(cps)
        g_x[e] = four(g_z).astype(BF16)
        return spread(
            "x", lambda k: g_x.at[e], lambda d, own: g_x.at[own], g_ss.at[pl.ds(7, 3)], g_rs.at[pl.ds(7, 3)]
        )

    def g_to_all(cps):
        arrive(cps)
        mine = y * 2 + core
        g_all[mine] = four(g_x) / live_total
        out = [send(g_all.at[mine], g_all.at[mine], g_ss.at[10], g_rs.at[10], sibling)]
        for d in (1, 2, 3):
            out.append(send(g_all.at[mine], g_all.at[mine], g_ss.at[10 + d], g_rs.at[10 + d], along["y"](d)))
        for d in (1, 2, 3):
            to = device(e, turn(y, d), z, 1 - core)
            out.append(send(g_all.at[mine], g_all.at[mine], g_ss.at[13 + d], g_rs.at[13 + d], to))
        started.extend(out)
        return out

    def g_finish(cps):
        arrive(cps)
        for k in range(8):
            gwout_out[:, k * LANES : (k + 1) * LANES] = g_all[k]

    order = [("y", "z"), ("z", "y")]

    def slot(first_axis, second_axis, first_index, second_index):
        return first_index * 4 + second_index if first_axis == "y" else second_index * 4 + first_index

    def to_core(j):
        def body(k, _):
            core_send[j, k] = acc[j, k * 2 + 1 - core].astype(BF16)
            return 0

        lax.fori_loop(0, 16, body, 0)
        cp = send(core_send.at[j], core_recv.at[j], p_ss.at[j, 0], p_rs.at[j, 0], sibling)
        started.append(cp)
        return [cp]

    def to_first(j, cps):
        arrive(cps)
        a, b = order[j]
        for p in range(4):
            def body(q, _):
                k = slot(a, b, p, q)
                one_send[j, p, q] = (acc[j, k * 2 + core] + core_recv[j, k].astype(F32)).astype(BF16)
                return 0

            lax.fori_loop(0, 4, body, 0)
        return spread(
            a, lambda k: one_send.at[j, k], lambda d, own: one_recv.at[j, d - 1],
            p_ss.at[j, pl.ds(1, 3)], p_rs.at[j, pl.ds(1, 3)],
        )

    def to_second(j, cps):
        arrive(cps)
        a, b = order[j]

        def body(q, _):
            total = one_send[j, place[a], q].astype(F32)
            for d in range(3):
                total = total + one_recv[j, d, q].astype(F32)
            two_send[j, q] = total.astype(BF16)
            return 0

        lax.fori_loop(0, 4, body, 0)
        return spread(
            b, lambda k: two_send.at[j, k], lambda d, own: two_recv.at[j, d - 1],
            p_ss.at[j, pl.ds(4, 3)], p_rs.at[j, pl.ds(4, 3)],
        )

    def to_x(j, cps):
        arrive(cps)
        total = two_send[j, place[order[j][1]]].astype(F32)
        for d in range(3):
            total = total + two_recv[j, d].astype(F32)
        three[j, e] = total.astype(BF16)
        return spread(
            "x", lambda k: three.at[j, e], lambda d, own: three.at[j, own],
            p_ss.at[j, pl.ds(7, 3)], p_rs.at[j, pl.ds(7, 3)],
        )

    def finish(j, cps):
        arrive(cps)
        gwin_out[:, j * WIDE : (j + 1) * WIDE] = four(three.at[j]) / live_total

    outs = []

    def latent_tile(t):
        m, s = t // 2, pl.ds((t % 2) * CHUNK, CHUNK)
        lat[m, s, :] = dot(back[m, s, :], w[...], 1, 1).astype(BF16)
        cp = pltpu.make_async_copy(lat.at[m, s], glat_hbm.at[m, s], out_sem.at[t])
        cp.start()
        outs.append(cp)

    g = g_start()
    acc[0] += weight_piece(1, 0)
    p0 = to_core(0)
    g = g_to_y(g)
    arrive([lc])
    ls_y[y] = ls_core[0] + ls_core[1]
    lc = spread("y", lambda k: ls_y.at[y], lambda d, own: ls_y.at[own], t_ss.at[pl.ds(8, 3)], t_rs.at[pl.ds(8, 3)])
    acc[1] += weight_piece(1, 1)
    p1 = to_core(1)
    p0 = to_first(0, p0)
    latent_tile(0)
    p1 = to_first(1, p1)
    g = g_to_z(g)
    arrive(lc)
    ls_z[z] = four(ls_y)
    lc = spread("z", lambda k: ls_z.at[z], lambda d, own: ls_z.at[own], t_ss.at[pl.ds(11, 3)], t_rs.at[pl.ds(11, 3)])
    latent_tile(1)
    latent_tile(2)
    g = g_to_x(g)
    arrive(lc)
    ls_x[e] = four(ls_z)
    lc = spread("x", lambda k: ls_x.at[e], lambda d, own: ls_x.at[own], t_ss.at[pl.ds(14, 3)], t_rs.at[pl.ds(14, 3)])
    latent_tile(3)
    p0 = to_second(0, p0)
    p1 = to_second(1, p1)
    g = g_to_all(g)
    arrive(lc)
    loss_out[...] = jnp.sum(four(ls_x), axis=1, keepdims=True) / weight_total + jnp.zeros((8, LANES), F32)
    p0 = to_x(0, p0)
    p1 = to_x(1, p1)
    g_finish(g)
    finish(0, p0)
    finish(1, p1)
    for cp in started:
        cp.wait_send()
    for cp in outs:
        cp.wait()


def per_device(latent, w_in, output_weight, targets, area_weights, live_counts):
    vmem = pl.BlockSpec(memory_space=pltpu.VMEM)
    hbm = pl.BlockSpec(memory_space=pl.ANY)
    V = pltpu.VMEM
    dma = pltpu.SemaphoreType.DMA
    scratch = [
        V((2, POINTS, FEATURES), BF16),
        V((FEATURES, FEATURES), BF16),
        V((2, POINTS, FEATURES), BF16),
        V((2, POINTS, FEATURES), BF16),
        V((PIECES, 32, ROWS, WIDE), F32),
        V((CHUNKS, 4, 2, VARS, LANES), BF16),
        V((CHUNKS, 4, 2, VARS, LANES), BF16),
        V((CHUNKS, 4, 2, VARS, LANES), BF16),
        V((CHUNKS, 4, 2, VARS, LANES), BF16),
        V((VARS, FEATURES), F32),
        V((8, LANES), F32),
        V((PIECES, 16, ROWS, WIDE), BF16),
        V((PIECES, 16, ROWS, WIDE), BF16),
        V((PIECES, 4, 4, ROWS, WIDE), BF16),
        V((PIECES, 3, 4, ROWS, WIDE), BF16),
        V((PIECES, 4, ROWS, WIDE), BF16),
        V((PIECES, 3, ROWS, WIDE), BF16),
        V((PIECES, 4, ROWS, WIDE), BF16),
        V((4, VARS, LANES), BF16),
        V((4, VARS, LANES), BF16),
        V((4, VARS, LANES), BF16),
        V((3, VARS, LANES), BF16),
        V((4, VARS, LANES), BF16),
        V((4, VARS, LANES), BF16),
        V((8, VARS, LANES), F32),
        V((2, 8, LANES), F32),
        V((4, 8, LANES), F32),
        V((4, 8, LANES), F32),
        V((2, 8, LANES), F32),
        V((4, 8, LANES), F32),
        V((4, 8, LANES), F32),
        V((4, 8, LANES), F32),
        dma((5,)), dma((4,)),
        dma((CHUNKS, 2, 3)), dma((CHUNKS, 2, 3)),
        dma((CHUNKS, 3)), dma((CHUNKS, 3)),
        dma((PIECES, 10)), dma((PIECES, 10)),
        dma((17,)), dma((17,)),
        dma((17,)), dma((17,)),
    ]
    loss, glat, gwin, gwout = pl.pallas_call(
        kernel,
        out_shape=[
            jax.ShapeDtypeStruct((8, LANES), F32),
            jax.ShapeDtypeStruct(latent.shape, BF16),
            jax.ShapeDtypeStruct((ROWS, FEATURES), F32),
            jax.ShapeDtypeStruct((VARS, FEATURES), F32),
        ],
        in_specs=[hbm, hbm, vmem, vmem, vmem, pl.BlockSpec(memory_space=pltpu.SMEM)],
        out_specs=[vmem, hbm, vmem, vmem],
        scratch_shapes=scratch,
        compiler_params=pltpu.CompilerParams(collective_id=1, has_side_effects=True, vmem_limit_bytes=56 << 20),
        name="energy_step",
    )(latent, w_in, output_weight, targets, area_weights.reshape(8, LANES), live_counts)
    return loss[0, 0], glat, gwin, gwout


def solution(mesh):
    placed = (P("ens", "sp", None), P(), P(), P(None, "sp"), P("sp"), P("sp"))
    return jax.shard_map(
        per_device,
        mesh=mesh,
        in_specs=placed,
        out_specs=(P(), P("ens", "sp", None), P("sp", None), P()),
        check_vma=False,
    )
```

time: 297 us -> 63.3 us (0.21)
  blocking collectives: 144 us -> 0 us
  waiting for transfers between devices: 76.2 us -> 0 us
  Pallas kernels: 0 us -> 54.5 us
  matrix products: 37.7 us -> 0 us
  between operations: 18 us -> 1.29 us
  other arithmetic: 8.8 us -> 0 us
  starting transfers between devices: 4.84 us -> 0 us
    psum x2 -> x0, blocking collectives: 134 us -> none  [the longest x1 68.5 us: per_device(): lax.psum(jnp.sum(weight_block * ensemble_skill_values), ('ens', 'sp'))]
    psum x1 -> x0, waiting for transfers between devices: 76.2 us -> none  [per_device(): input_sum, output_sum = lax.psum((input_term, head_term), ('ens', 'sp'))]
    pallas_call x0 -> x1, Pallas kernels: none -> 54.5 us  [per_device(): pl.pallas_call(kernel, out_shape=[jax.ShapeDtypeStruct((8, LANES), F32),...]
    dot_general x6 -> x0, matrix products: 37.7 us -> none  [the longest x1 10.8 us: per_device(): jnp.einsum('mph,hk->mpk', latent, w_in, preferred_element_type=jnp.float32)]
    all_to_all x1 -> x0, blocking collectives: 10.5 us -> none  [per_device(): lax.all_to_all(derivative_coefficients.astype(jnp.bfloat16), 'ens', split...]
    div x3 -> x0, other arithmetic: 5 us -> none  [the longest x1 2.41 us: per_device(): output_sum / live_total]
    all_to_all x1 -> x0, starting transfers between devices: 4.84 us -> none  [per_device(): lax.all_to_all(ensemble_prediction, 'ens', split_axis=2, concat_axis=0, t...]
    unnamed x15 -> x7, local copies, waits for them, and re-layouts: 4.44 us -> 6.08 us
  transfers between devices with their start and end apart: 2 -> 0, of which waited for: 1 -> 0; matrix products, arithmetic and copies ran while one was open for 4% -> 0% of each run, Pallas kernels for 0% -> 0%
where the time goes in v1:
time: 63.3 us; the launch traced here: 63.1 us
  Pallas kernels  54.5 us (86%)
  local copies, waits for them, and re-layouts  7.27 us (11%)
  between operations  1.29 us (2%)
    pallas_call x1, Pallas kernels, per_device(): pl.pallas_call(kernel, out_shape=[jax.ShapeDtypeStruct((8, LANES), F32),...  54.5 us
    unnamed x7, local copies, waits for them, and re-layouts  6.08 us

profile of v1, /device:TPU:1, one launch (start us, length us, event | category | flops | bytes accessed | tf_op | source)
XLA Modules:
  0.0 63.1 jit_solution(4570685593536478986)
XLA Ops:
  1.3 54.5 %energy_step.1 = (f32[8,128]{1,0:T(8,128)}, bf16[2,1024,1024]{2,1,0:T(8,128)(2,1)}, f32[32,1024]{1,0:T(8,128)}, f32[80,1024]{1,0:T(8,128)}) custom-call(bf16[2,1024,1024]{2,1,0:T(8,128)(2,1)} %lat_hbm.1, bf16[1024,1024]{1,0:T(8,128)(2,1)} %w_hbm.1, bf16[80,1024]{1,0:T(8,128)(2,1)} %wout.1, bf16[80,1024]{1,0:T(8,128)(2,1)} %targets.1, f32[8,128]{1,0:T(8,128)} %bitcast.2, ...), custom_call_target="tpu_custom_call" | custom-call | tf_op jit(solution)/shard_map/energy_step/pallas_call | solution.py:454
  55.8 1.2 %slice.3 = f32[1,1]{1,0:T(1,128)} slice(f32[8,128]{1,0:T(8,128)} %get-tuple-element.8), slice={[0:1], [0:1]} | slice | bytes 8 | tf_op jit(solution)/shard_map/slice | solution.py:468
  57.0 0.0 copy-start.1
  57.0 0.0 copy-start
  57.0 4.7 %copy.14 = bf16[2,1024,1024]{2,1,0:T(8,128)(2,1)} copy(bf16[2,1024,1024]{2,1,0:T(8,128)(2,1)} %get-tuple-element.17) | data formatting | bytes 8388608
  61.7 0.0 copy-done.1
  61.7 0.7 %copy.15 = f32[32,1024]{1,0:T(8,128)} copy(f32[32,1024]{1,0:T(8,128)S(1)} %copy-done.1) | data formatting | bytes 262144
  62.4 0.0 copy-done
  62.4 0.7 %copy.16 = f32[80,1024]{1,0:T(8,128)} copy(f32[80,1024]{1,0:T(8,128)S(1)} %copy-done) | data formatting | bytes 655360
Async XLA Ops:
  57.0 4.7 %copy-start.1 = (f32[32,1024]{1,0:T(8,128)S(1)}, f32[32,1024]{1,0:T(8,128)}, u32[]{:S(2)}) copy-start(f32[32,1024]{1,0:T(8,128)} %get-tuple-element.18) | copy-start | bytes 393220
  57.0 5.4 %copy-start = (f32[80,1024]{1,0:T(8,128)S(1)}, f32[80,1024]{1,0:T(8,128)}, u32[]{:S(2)}) copy-start(f32[80,1024]{1,0:T(8,128)} %get-tuple-element.19) | copy-start | bytes 983044

commit v2 on v1

v2 whole, which is shorter than its diff:
```python
import functools
import math

import jax
import jax.numpy as jnp
from jax import lax
from jax.experimental import pallas as pl
from jax.experimental.pallas import tpu as pltpu
from jax.sharding import PartitionSpec as P

BF16, F32 = jnp.bfloat16, jnp.float32
MESH = pl.DeviceIdType.MESH
LOSS_SCALE = 1024.0
MEMBERS, VARS, FEATURES, POINTS = 8, 80, 1024, 1024
CHUNKS = 2
CHUNK = POINTS // CHUNKS
LANES = 128
PIECES = 4
WIDE = FEATURES // PIECES
ROWS = 32
OUTER = math.sqrt(2.0 / math.pi)
INNER = OUTER * 0.044715


def dot(a, b, ca, cb):
    return lax.dot_general(a, b, (((ca,), (cb,)), ((), ())), preferred_element_type=F32)


def activation(z):
    cubic = INNER * (z * z)
    s = 0.5 * jnp.tanh(z * (cubic + OUTER)) + 0.5
    h = z * s
    slope = s + (h - h * s) * (6.0 * cubic + 2.0 * OUTER)
    return h.astype(BF16), slope.astype(BF16)


def activation_only(z):
    return (z * (0.5 * jnp.tanh(z * (INNER * (z * z) + OUTER)) + 0.5)).astype(BF16)


def score_block(x_ref, y, weighted, scales, store):
    n = MEMBERS
    pairs = [(i, j) for i in range(n) for j in range(i + 1, n)]
    step = 16
    own = [jnp.zeros((step, LANES), F32) for _ in range(n)]
    between = [jnp.zeros((step, LANES), F32) for _ in pairs]
    for v in range(0, VARS, step):
        x = [x_ref[m // 2, m % 2, v : v + step, :].astype(F32) for m in range(n)]
        for m in range(n):
            d = x[m] - y[v : v + step]
            own[m] = own[m] + d * d
        for q, (i, j) in enumerate(pairs):
            d = x[i] - x[j]
            between[q] = between[q] + d * d
    a = [jnp.sqrt(jnp.sum(o, axis=0, keepdims=True) + 1.0) for o in own]
    b = [jnp.sqrt(jnp.sum(o, axis=0, keepdims=True) + 1.0) for o in between]
    score = sum(a) / n - sum(b) / (n * (n - 1.0))
    from_target = [scales / (n * t) for t in a]
    from_pair = [scales / (n * (n - 1.0) * t) for t in b]
    for v in range(0, VARS, step):
        x = [x_ref[m // 2, m % 2, v : v + step, :].astype(F32) for m in range(n)]
        total = [(x[m] - y[v : v + step]) * from_target[m] for m in range(n)]
        for q, (i, j) in enumerate(pairs):
            d = (x[i] - x[j]) * from_pair[q]
            total[i] = total[i] - d
            total[j] = total[j] + d
        for m in range(n):
            store(m, v, step, total[m].astype(BF16))
    return weighted * score


def kernel(
    lat_hbm, w_hbm, wout_hbm, targets_hbm, area_hbm, live,
    loss_out, glat_out, gwin_out, gwout_out,
    lat, later, w, wout, targets, area, hid, back, acc, fsend, frecv, ssend, srecv, gout,
    core_send, core_recv, one_send, one_recv, two_send, two_recv, three,
    g_core_send, g_core_recv, g_y_send, g_y_recv, g_z, g_x, g_all,
    wt_near, wt_y, ls_core, ls_y, ls_z, ls_x,
    in_sem, f_ss, f_rs, s_ss, s_rs, p_ss, p_rs, g_ss, g_rs, t_ss, t_rs,
):
    e = lax.axis_index("ens")
    sp = lax.axis_index("sp")
    core = lax.rem(sp, 2)
    z = lax.rem(sp // 2, 4)
    y = sp // 8

    def turn(i, d):
        return lax.rem(i + d, 4)

    def device(x_, y_, z_, core_):
        return (x_, (y_ * 4 + z_) * 2 + core_)

    along = {
        "x": lambda d: device(turn(e, d), y, z, core),
        "y": lambda d: device(e, turn(y, d), z, core),
        "z": lambda d: device(e, y, turn(z, d), core),
    }
    place = {"x": e, "y": y, "z": z}
    sibling = device(e, y, z, 1 - core)

    def load(m, c):
        s = pl.ds(c * CHUNK, CHUNK)
        return pltpu.make_async_copy(lat_hbm.at[m, s], lat.at[m, s], in_sem.at[1 + 2 * c + m])

    load_w = [
        pltpu.make_async_copy(w_hbm.at[pl.ds(i * 256, 256)], w.at[pl.ds(i * 256, 256)], in_sem.at[8 + i])
        for i in range(4)
    ]
    for cp in load_w:
        cp.start()
    load(0, 0).start()
    small = [
        pltpu.make_async_copy(a, b, in_sem.at[5 + i])
        for i, (a, b) in enumerate([(area_hbm, area), (wout_hbm, wout), (targets_hbm, targets)])
    ]
    for cp in small:
        cp.start()
    loads = {(c, m): load(m, c) for c in range(CHUNKS) for m in range(2)}

    peers = [along[k](d) for k in "xyz" for d in (1, 2, 3)] + [sibling]
    peers += [device(turn(e, d), y, z, 1 - core) for d in (1, 2, 3)]
    across_z = [device(e, y, turn(z, d), 1 - core) for d in (1, 2, 3)]
    peers += across_z
    barrier = pltpu.get_barrier_semaphore()
    for p in peers:
        pl.semaphore_signal(barrier, inc=1, device_id=p, device_id_type=MESH)

    def send(src, dst, ss, rs, to):
        cp = pltpu.make_async_remote_copy(
            src_ref=src, dst_ref=dst, send_sem=ss, recv_sem=rs, device_id=to, device_id_type=MESH
        )
        cp.start()
        return cp

    started = []

    def spread(axis, src, dst, ss, rs, hops=(2, 1, 3)):
        cps = []
        for d in hops:
            cps.append(send(src(turn(place[axis], d)), dst(d, place[axis]), ss.at[d - 1], rs.at[d - 1], along[axis](d)))
        started.extend(cps)
        return cps

    def four(ref):
        return (ref[0].astype(F32) + ref[1].astype(F32)) + (ref[2].astype(F32) + ref[3].astype(F32))

    def arrive(cps):
        for cp in cps:
            cp.wait_recv()

    for cp in small:
        cp.wait()
    where = lax.broadcasted_iota(jnp.int32, (8, LANES), 0) * LANES + lax.broadcasted_iota(jnp.int32, (8, LANES), 1)
    is_live = (where < live[0]).astype(F32)
    weighted_all = area[...] * is_live
    first = lax.broadcasted_iota(jnp.int32, (8, LANES), 0) == 0
    wt_own = jnp.where(
        first, jnp.sum(weighted_all, axis=0, keepdims=True), jnp.sum(is_live, axis=0, keepdims=True)
    )
    wt_near[z * 2 + core] = wt_own

    def forward(c, m):
        s = pl.ds(c * CHUNK, CHUNK)
        pre = jnp.dot(lat[m, s, :], w[...], preferred_element_type=F32)
        if c == 0:
            hid[m, s, :], back[m, s, :] = activation(pre)
        else:
            hid[m, s, :] = activation_only(pre)
            later[m] = pre
        f = dot(wout[...], hid[m, s, :], 1, 1).astype(BF16)
        for k in range(4):
            fsend[c, k, m] = f[:, k * LANES : (k + 1) * LANES]
        frecv[c, e, m] = fsend[c, e, m]

    def forward_send(c, m, hops=(2, 1, 3)):
        return spread(
            "x", lambda k: fsend.at[c, k, m], lambda d, own: frecv.at[c, own, m], f_ss.at[c, m], f_rs.at[c, m], hops
        )

    def forward_half(c, m, hops):
        rows = [pl.ds(pl.multiple_of(c * CHUNK + turn(e, d) * LANES, LANES), LANES) for d in hops]
        pre = jnp.dot(
            jnp.concatenate([lat[m, r, :] for r in rows], axis=0), w[...], preferred_element_type=F32
        )
        h = activation_only(pre)
        for i, (r, d) in enumerate(zip(rows, hops)):
            hid[m, r, :] = h[i * LANES : (i + 1) * LANES]
            to = pl.ds(pl.multiple_of(turn(e, d) * LANES, LANES), LANES)
            later[m, to, :] = pre[i * LANES : (i + 1) * LANES]
        f = dot(wout[...], h, 1, 1).astype(BF16)
        for i, d in enumerate(hops):
            fsend[c, turn(e, d), m] = f[:, i * LANES : (i + 1) * LANES]

    loss_rows = []

    def scored(c):
        block = c * 4 + e
        y_block = targets[:, pl.ds(pl.multiple_of(block * LANES, LANES), LANES)].astype(F32)
        lanes = lax.broadcasted_iota(jnp.int32, (1, LANES), 1)
        weighted = area[pl.ds(block, 1), :] * (block * LANES + lanes < live[0]).astype(F32)
        scales = LOSS_SCALE * live_total * weighted / weight_total

        def store(m, v, step, value):
            ssend[c, m // 2, m % 2, v : v + step, :] = value

        loss_rows.append(score_block(frecv.at[c], y_block, weighted, scales, store))
        srecv[c, e] = ssend[c, e]
        return spread("x", lambda k: ssend.at[c, k], lambda d, own: srecv.at[c, own], s_ss.at[c], s_rs.at[c])

    def backward(c):
        s = pl.ds(c * CHUNK, CHUNK)
        for m in range(2):
            slopes = jnp.concatenate([srecv[c, k, m] for k in range(4)], axis=1)
            bh = dot(slopes, wout[...], 0, 0)
            back[m, s, :] = (back[m, s, :].astype(F32) * bh).astype(BF16)

    def output_part(c):
        s = pl.ds(c * CHUNK, CHUNK)
        slopes = jnp.concatenate([srecv[c, k, m] for m in range(2) for k in range(4)], axis=1)
        return dot(slopes, hid[:, s, :].reshape(2 * CHUNK, FEATURES), 1, 0)

    def weight_pieces(c, i):
        s, lo = pl.ds(c * CHUNK, CHUNK), 2 * i * WIDE
        a = lat[:, s, :].reshape(2 * CHUNK, FEATURES)
        both = dot(a, back[:, s, lo : lo + 2 * WIDE].reshape(2 * CHUNK, 2 * WIDE), 0, 0)
        for k in range(2):
            term = both[:, k * WIDE : (k + 1) * WIDE].reshape(16, 2, ROWS, WIDE)
            if c == 0:
                acc[2 * i + k] = term
            else:
                acc[2 * i + k] += term

    def g_start():
        def body(k, _):
            cols = pl.ds(pl.multiple_of((k * 2 + 1 - core) * LANES, LANES), LANES)
            g_core_send[k] = gout[:, cols].astype(BF16)
            return 0

        lax.fori_loop(0, 4, body, 0)
        cp = send(g_core_send, g_core_recv, g_ss.at[0], g_rs.at[0], sibling)
        started.append(cp)
        return [cp]

    def g_to_first(cps):
        arrive(cps)

        def body(k, _):
            cols = pl.ds(pl.multiple_of((k * 2 + core) * LANES, LANES), LANES)
            g_y_send[k] = (gout[:, cols] + g_core_recv[k].astype(F32)).astype(BF16)
            return 0

        lax.fori_loop(0, 4, body, 0)
        return spread(
            "x", lambda k: g_y_send.at[k], lambda d, own: g_y_recv.at[d - 1], g_ss.at[pl.ds(1, 3)], g_rs.at[pl.ds(1, 3)]
        )

    def g_to_second(cps):
        arrive(cps)
        total = g_y_send[e].astype(F32)
        for d in range(3):
            total = total + g_y_recv[d].astype(F32)
        g_z[y] = total.astype(BF16)
        return spread(
            "y", lambda k: g_z.at[y], lambda d, own: g_z.at[own], g_ss.at[pl.ds(4, 3)], g_rs.at[pl.ds(4, 3)]
        )

    def g_to_third(cps):
        arrive(cps)
        g_x[z] = four(g_z).astype(BF16)
        return spread(
            "z", lambda k: g_x.at[z], lambda d, own: g_x.at[own], g_ss.at[pl.ds(7, 3)], g_rs.at[pl.ds(7, 3)]
        )

    def g_to_all(cps):
        arrive(cps)
        mine = e * 2 + core
        g_all[mine] = (four(g_x) / live_total).astype(BF16)
        out = [send(g_all.at[mine], g_all.at[mine], g_ss.at[10], g_rs.at[10], sibling)]
        for d in (1, 2, 3):
            out.append(send(g_all.at[mine], g_all.at[mine], g_ss.at[10 + d], g_rs.at[10 + d], along["x"](d)))
        for d in (1, 2, 3):
            to = device(turn(e, d), y, z, 1 - core)
            out.append(send(g_all.at[mine], g_all.at[mine], g_ss.at[13 + d], g_rs.at[13 + d], to))
        started.extend(out)
        return out

    def g_finish(cps):
        arrive(cps)
        for k in range(8):
            gwout_out[:, k * LANES : (k + 1) * LANES] = g_all[k].astype(F32)

    order = [("y", "z"), ("z", "y")] * (PIECES // 2)

    def to_core(j):
        core_send[j] = acc[j, :, 1 - core].astype(BF16)
        cp = send(core_send.at[j], core_recv.at[j], p_ss.at[j, 0], p_rs.at[j, 0], sibling)
        started.append(cp)
        return [cp]

    def part(j, k):
        return one_send.at[j, k] if order[j][0] == "y" else one_send.at[j, :, k]

    def to_first(j, cps):
        arrive(cps)
        one_send[j] = (acc[j, :, core] + core_recv[j].astype(F32)).astype(BF16).reshape(4, 4, ROWS, WIDE)
        return spread(
            order[j][0], lambda k: part(j, k), lambda d, own: one_recv.at[j, d - 1],
            p_ss.at[j, pl.ds(1, 3)], p_rs.at[j, pl.ds(1, 3)],
        )

    def to_second(j, cps):
        arrive(cps)
        total = part(j, place[order[j][0]])[...].astype(F32)
        for d in range(3):
            total = total + one_recv[j, d].astype(F32)
        two_send[j] = total.astype(BF16)
        return spread(
            order[j][1], lambda k: two_send.at[j, k], lambda d, own: two_recv.at[j, d - 1],
            p_ss.at[j, pl.ds(4, 3)], p_rs.at[j, pl.ds(4, 3)],
        )

    def to_x(j, cps):
        arrive(cps)
        total = two_send[j, place[order[j][1]]].astype(F32)
        for d in range(3):
            total = total + two_recv[j, d].astype(F32)
        three[j, e] = total.astype(BF16)
        return spread(
            "x", lambda k: three.at[j, e], lambda d, own: three.at[j, own],
            p_ss.at[j, pl.ds(7, 3)], p_rs.at[j, pl.ds(7, 3)],
        )

    def finish(j, cps):
        arrive(cps)
        gwin_out[:, j * WIDE : (j + 1) * WIDE] = four(three.at[j]) / live_total

    def latent_tile(t):
        m, s = t // 2, pl.ds((t % 2) * CHUNK, CHUNK)
        glat_out[m, s, :] = dot(back[m, s, :], w[...], 1, 1).astype(BF16)

    for cp in load_w:
        cp.wait()
    loads[0, 0].wait()
    for key in ((0, 1), (1, 0), (1, 1)):
        loads[key].start()
    forward(0, 0)
    pl.semaphore_wait(barrier, len(peers))
    f00 = forward_send(0, 0)
    mine = z * 2 + core
    tw = []
    for i, to in enumerate([sibling] + [along["z"](d) for d in (1, 2, 3)] + across_z):
        tw.append(send(wt_near.at[mine], wt_near.at[mine], t_ss.at[17 + i], t_rs.at[17 + i], to))
    started.extend(tw)
    loads[0, 1].wait()
    forward(0, 1)
    f01 = forward_send(0, 1)
    arrive(tw)
    near = wt_near[0]
    for i in range(1, 8):
        near = near + wt_near[i]
    wt_y[y] = near
    tw = spread("y", lambda k: wt_y.at[y], lambda d, own: wt_y.at[own], t_ss.at[pl.ds(4, 3)], t_rs.at[pl.ds(4, 3)])
    loads[1, 0].wait()
    forward(1, 0)
    f10 = forward_send(1, 0)
    loads[1, 1].wait()
    forward_half(1, 1, (2, 1))
    f11 = forward_send(1, 1, (2, 1))
    arrive(tw)
    totals = jnp.sum(four(wt_y), axis=1, keepdims=True)
    weight_total = totals[0:1, 0:1]
    live_total = totals[1:2, 0:1]
    arrive(f00)
    arrive(f01)
    s0 = scored(0)
    forward_half(1, 1, (3, 0))
    f11 += forward_send(1, 1, (3,))
    frecv[1, e, 1] = fsend[1, e, 1]
    for m in range(2):
        back[m, CHUNK:, :] = activation(later[m])[1]
    arrive(f10)
    arrive(f11)
    s1 = scored(1)
    ls_core[core] = jnp.broadcast_to(loss_rows[0] + loss_rows[1], (8, LANES))
    lc = send(ls_core.at[core], ls_core.at[core], t_ss.at[7], t_rs.at[7], sibling)
    started.append(lc)
    arrive(s0)
    backward(0)
    gout[...] = output_part(0)
    arrive([lc])
    ls_y[y] = ls_core[0] + ls_core[1]
    lc = spread("y", lambda k: ls_y.at[y], lambda d, own: ls_y.at[own], t_ss.at[pl.ds(8, 3)], t_rs.at[pl.ds(8, 3)])
    weight_pieces(0, 0)
    weight_pieces(0, 1)
    arrive(s1)
    gout[...] += output_part(1)
    g = g_start()
    backward(1)
    g = g_to_first(g)
    weight_pieces(1, 0)
    p0 = to_core(0)
    p1 = to_core(1)
    arrive(lc)
    ls_z[z] = four(ls_y)
    lc = spread("z", lambda k: ls_z.at[z], lambda d, own: ls_z.at[own], t_ss.at[pl.ds(11, 3)], t_rs.at[pl.ds(11, 3)])
    weight_pieces(1, 1)
    p2 = to_core(2)
    p3 = to_core(3)
    g = g_to_second(g)
    p0 = to_first(0, p0)
    p1 = to_first(1, p1)
    latent_tile(0)
    p2 = to_first(2, p2)
    p3 = to_first(3, p3)
    latent_tile(1)
    g = g_to_third(g)
    arrive(lc)
    ls_x[e] = four(ls_z)
    lc = spread("x", lambda k: ls_x.at[e], lambda d, own: ls_x.at[own], t_ss.at[pl.ds(14, 3)], t_rs.at[pl.ds(14, 3)])
    latent_tile(2)
    p0 = to_second(0, p0)
    p1 = to_second(1, p1)
    latent_tile(3)
    p2 = to_second(2, p2)
    p3 = to_second(3, p3)
    g = g_to_all(g)
    arrive(lc)
    loss_out[...] = jnp.sum(four(ls_x), axis=1, keepdims=True) / weight_total + jnp.zeros((8, LANES), F32)
    p0 = to_x(0, p0)
    p1 = to_x(1, p1)
    p2 = to_x(2, p2)
    p3 = to_x(3, p3)
    g_finish(g)
    finish(0, p0)
    finish(1, p1)
    finish(2, p2)
    finish(3, p3)
    for cp in started:
        cp.wait_send()


def write_out(loss, glat, gwin, gwout, loss_out, glat_out, gwin_out, gwout_out, sem):
    cps = [pltpu.make_async_copy(gwin, gwin_out, sem.at[0]), pltpu.make_async_copy(gwout, gwout_out, sem.at[1])]
    for i in range(16):
        m, s = i // 8, pl.ds((i % 8) * LANES, LANES)
        cps.append(pltpu.make_async_copy(glat.at[m, s], glat_out.at[m, s], sem.at[2 + i]))
    for cp in cps:
        cp.start()
    loss_out[...] = loss[0:1, 0:1]
    for cp in cps:
        cp.wait()


def per_device(latent, w_in, output_weight, targets, area_weights, live_counts):
    vmem = pl.BlockSpec(memory_space=pltpu.VMEM)
    hbm = pl.BlockSpec(memory_space=pl.ANY)
    V = pltpu.VMEM
    dma = pltpu.SemaphoreType.DMA
    scratch = [
        V((2, POINTS, FEATURES), BF16),
        V((2, CHUNK, FEATURES), F32),
        V((FEATURES, FEATURES), BF16),
        V((VARS, FEATURES), BF16),
        V((VARS, POINTS), BF16),
        V((8, LANES), F32),
        V((2, POINTS, FEATURES), BF16),
        V((2, POINTS, FEATURES), BF16),
        V((PIECES, 16, 2, ROWS, WIDE), F32),
        V((CHUNKS, 4, 2, VARS, LANES), BF16),
        V((CHUNKS, 4, 2, VARS, LANES), BF16),
        V((CHUNKS, 4, 2, VARS, LANES), BF16),
        V((CHUNKS, 4, 2, VARS, LANES), BF16),
        V((VARS, FEATURES), F32),
        V((PIECES, 16, ROWS, WIDE), BF16),
        V((PIECES, 16, ROWS, WIDE), BF16),
        V((PIECES, 4, 4, ROWS, WIDE), BF16),
        V((PIECES, 3, 4, ROWS, WIDE), BF16),
        V((PIECES, 4, ROWS, WIDE), BF16),
        V((PIECES, 3, ROWS, WIDE), BF16),
        V((PIECES, 4, ROWS, WIDE), BF16),
        V((4, VARS, LANES), BF16),
        V((4, VARS, LANES), BF16),
        V((4, VARS, LANES), BF16),
        V((3, VARS, LANES), BF16),
        V((4, VARS, LANES), BF16),
        V((4, VARS, LANES), BF16),
        V((8, VARS, LANES), BF16),
        V((8, 8, LANES), F32),
        V((4, 8, LANES), F32),
        V((2, 8, LANES), F32),
        V((4, 8, LANES), F32),
        V((4, 8, LANES), F32),
        V((4, 8, LANES), F32),
        dma((12,)),
        dma((CHUNKS, 2, 3)), dma((CHUNKS, 2, 3)),
        dma((CHUNKS, 3)), dma((CHUNKS, 3)),
        dma((PIECES, 10)), dma((PIECES, 10)),
        dma((17,)), dma((17,)),
        dma((24,)), dma((24,)),
    ]
    operands = (latent, w_in, output_weight, targets, area_weights.reshape(8, LANES))
    results = pl.pallas_call(
        kernel,
        out_shape=[
            V((8, LANES), F32),
            V(latent.shape, BF16),
            V((ROWS, FEATURES), F32),
            V((VARS, FEATURES), F32),
        ],
        in_specs=[pl.BlockSpec(memory_space=pltpu.HBM)] * 5 + [pl.BlockSpec(memory_space=pltpu.SMEM)],
        out_specs=[vmem] * 4,
        scratch_shapes=scratch,
        compiler_params=pltpu.CompilerParams(collective_id=1, has_side_effects=True, vmem_limit_bytes=48 << 20),
        name="energy_step",
    )(*[pltpu.with_memory_space_constraint(a, pltpu.HBM) for a in operands], live_counts)
    loss, glat, gwin, gwout = pl.pallas_call(
        write_out,
        out_shape=[
            jax.ShapeDtypeStruct((1, 1), F32),
            jax.ShapeDtypeStruct(latent.shape, BF16),
            jax.ShapeDtypeStruct((ROWS, FEATURES), F32),
            jax.ShapeDtypeStruct((VARS, FEATURES), F32),
        ],
        in_specs=[vmem] * 4,
        out_specs=[vmem] + [hbm] * 3,
        scratch_shapes=[dma((18,))],
        compiler_params=pltpu.CompilerParams(vmem_limit_bytes=1 << 20),
        name="write_out",
    )(*[pltpu.with_memory_space_constraint(r, pltpu.VMEM) for r in results])
    return loss.reshape(()), glat, gwin, gwout


def solution(mesh):
    placed = (P("ens", "sp", None), P(), P(), P(None, "sp"), P("sp"), P("sp"))
    return jax.shard_map(
        per_device,
        mesh=mesh,
        in_specs=placed,
        out_specs=(P(), P("ens", "sp", None), P("sp", None), P()),
        check_vma=False,
    )
```

time: 63.3 us -> 54.4 us (0.86)
  local copies, waits for them, and re-layouts: 7.27 us -> 0 us
  Pallas kernels: 54.5 us -> 52.8 us
    unnamed x7 -> x0, local copies, waits for them, and re-layouts: 6.08 us -> none
    pallas_call x1 -> x2, Pallas kernels: 54.5 us -> 52.8 us  [the longest x1 50 us: per_device(): pl.pallas_call(kernel, out_shape=[V((8, LANES), F32), V(latent.shape, BF1...]
    slice x1 -> x0, local copies, waits for them, and re-layouts: 1.19 us -> none  [per_device(): return (loss[0, 0], glat, gwin, gwout)]
where the time goes in v2:
time: 54.4 us; the launch traced here: 54.3 us
  Pallas kernels  52.8 us (97%)
  between operations  1.45 us (3%)
    pallas_call x1, Pallas kernels, per_device(): pl.pallas_call(kernel, out_shape=[V((8, LANES), F32), V(latent.shape, BF1...  50 us
    pallas_call x1, Pallas kernels, per_device(): pl.pallas_call(write_out, out_shape=[jax.ShapeDtypeStruct((1, 1), F32), j...  2.81 us

profile of v2, /device:TPU:1, one launch (start us, length us, event | category | flops | bytes accessed | tf_op | source)
XLA Modules:
  0.0 54.3 jit_solution(11414734377474851693)
XLA Ops:
  1.3 50.0 %energy_step.1 = (f32[8,128]{1,0:T(8,128)S(1)}, bf16[2,1024,1024]{2,1,0:T(8,128)(2,1)S(1)}, f32[32,1024]{1,0:T(8,128)S(1)}, f32[80,1024]{1,0:T(8,128)S(1)}) custom-call(bf16[2,1024,1024]{2,1,0:T(8,128)(2,1)} %lat_hbm.1, bf16[1024,1024]{1,0:T(8,128)(2,1)} %w_hbm.1, bf16[80,1024]{1,0:T(8,128)(2,1)} %wout_hbm.1, bf16[80,1024]{1,0:T(8,128)(2,1)} %targets_hbm.1, ...), custom_call_target="tpu_custom_call" | custom-call | tf_op jit(solution)/shard_map/energy_step/pallas_call | solution.py:502
  51.3 2.8 %write_out.1 = (f32[1,1]{1,0:T(1,128)}, bf16[2,1024,1024]{2,1,0:T(8,128)(2,1)}, f32[32,1024]{1,0:T(8,128)}, f32[80,1024]{1,0:T(8,128)}) custom-call(f32[8,128]{1,0:T(8,128)S(1)} %get-tuple-element.12.loss, bf16[2,1024,1024]{2,1,0:T(8,128)(2,1)S(1)} %get-tuple-element.13.glat, f32[32,1024]{1,0:T(8,128)S(1)} %get-tuple-element.14.gwin, ...), custom_call_target="tpu_custom_call" | custom-call | tf_op jit(solution)/shard_map/write_out/pallas_call | solution.py:516

commit v3 on v2

v3 whole, which is shorter than its diff:
```python
import functools
import math

import jax
import jax.numpy as jnp
from jax import lax
from jax.experimental import pallas as pl
from jax.experimental.pallas import tpu as pltpu
from jax.sharding import PartitionSpec as P

BF16, F32 = jnp.bfloat16, jnp.float32
MESH = pl.DeviceIdType.MESH
LOSS_SCALE = 1024.0
MEMBERS, VARS, FEATURES, POINTS = 8, 80, 1024, 1024
CHUNKS = 2
CHUNK = POINTS // CHUNKS
LANES = 128
HALF = FEATURES // 2
PIECES = ((0, 256, 128, "y"), (0, 384, 128, "z"), (1, 0, 256, "y"), (1, 256, 256, "z"))
SENDS = 8
FAR = ((2, 2), (2, 1), (2, 3), (1, 2), (3, 2))
ROWS = 32
OUTER = math.sqrt(2.0 / math.pi)
INNER = OUTER * 0.044715


def dot(a, b, ca, cb):
    return lax.dot_general(a, b, (((ca,), (cb,)), ((), ())), preferred_element_type=F32)


def activation(z):
    cubic = INNER * (z * z)
    s = 0.5 * jnp.tanh(z * (cubic + OUTER)) + 0.5
    h = z * s
    slope = s + (h - h * s) * (6.0 * cubic + 2.0 * OUTER)
    return h.astype(BF16), slope.astype(BF16)


def activation_only(z):
    return (z * (0.5 * jnp.tanh(z * (INNER * (z * z) + OUTER)) + 0.5)).astype(BF16)


def score_block(x_ref, y, weighted, scales, store):
    n = MEMBERS
    pairs = [(i, j) for i in range(n) for j in range(i + 1, n)]
    step = 16
    own = [jnp.zeros((step, LANES), F32) for _ in range(n)]
    between = [jnp.zeros((step, LANES), F32) for _ in pairs]
    for v in range(0, VARS, step):
        x = [x_ref[m // 2, m % 2, v : v + step, :].astype(F32) for m in range(n)]
        for m in range(n):
            d = x[m] - y[v : v + step]
            own[m] = own[m] + d * d
        for q, (i, j) in enumerate(pairs):
            d = x[i] - x[j]
            between[q] = between[q] + d * d
    a = [jnp.sqrt(jnp.sum(o, axis=0, keepdims=True) + 1.0) for o in own]
    b = [jnp.sqrt(jnp.sum(o, axis=0, keepdims=True) + 1.0) for o in between]
    score = sum(a) / n - sum(b) / (n * (n - 1.0))
    from_target = [scales / (n * t) for t in a]
    from_pair = [scales / (n * (n - 1.0) * t) for t in b]
    for v in range(0, VARS, step):
        x = [x_ref[m // 2, m % 2, v : v + step, :].astype(F32) for m in range(n)]
        total = [(x[m] - y[v : v + step]) * from_target[m] for m in range(n)]
        for q, (i, j) in enumerate(pairs):
            d = (x[i] - x[j]) * from_pair[q]
            total[i] = total[i] - d
            total[j] = total[j] + d
        for m in range(n):
            store(m, v, step, total[m].astype(BF16))
    return weighted * score


def kernel(
    lat_hbm, w_hbm, wout_hbm, targets_hbm, area_hbm, live,
    loss_out, glat_out, gwin_out, gwout_out,
    lat, later, w, wout, targets, area, hid, back, acc, fsend, frecv, ssend, srecv, gout,
    core_send, core_recv, one_send, one_recv, two_send, two_recv, three,
    x_send, x_recv, xy_send, xy_recv, xz_send, x_all,
    g_core_send, g_core_recv, g_one_send, g_one_recv, g_two, g_three, g_all,
    wt_near, wt_y, ls_core, ls_y, ls_z, ls_x,
    in_sem, out_sem, f_rs, s_rs, p_rs, g_rs, t_rs,
):
    e = lax.axis_index("ens")
    sp = lax.axis_index("sp")
    core = lax.rem(sp, 2)
    z = lax.rem(sp // 2, 4)
    y = sp // 8

    def turn(i, d):
        return lax.rem(i + d, 4)

    def device(x_, y_, z_, core_):
        return (x_, (y_ * 4 + z_) * 2 + core_)

    along = {
        "x": lambda d: device(turn(e, d), y, z, core),
        "y": lambda d: device(e, turn(y, d), z, core),
        "z": lambda d: device(e, y, turn(z, d), core),
    }
    place = {"x": e, "y": y, "z": z}
    sibling = device(e, y, z, 1 - core)
    across_x = [device(turn(e, d), y, z, 1 - core) for d in (1, 2, 3)]
    across_z = [device(e, y, turn(z, d), 1 - core) for d in (1, 2, 3)]

    def load(m, c):
        s = pl.ds(c * CHUNK, CHUNK)
        return pltpu.make_async_copy(lat_hbm.at[m, s], lat.at[m, s], in_sem.at[2 * c + m])

    loads = {(c, m): load(m, c) for c in range(CHUNKS) for m in range(2)}
    loads[0, 0].start()
    load_w = []
    for i in range(2):
        cols = pl.ds(i * HALF, HALF)
        load_w.append(pltpu.make_async_copy(w_hbm.at[:, cols], w.at[:, cols], in_sem.at[4 + i]))
        load_w[i].start()
    small = [
        pltpu.make_async_copy(src, dst, in_sem.at[8 + i])
        for i, (src, dst) in enumerate([(area_hbm, area), (wout_hbm, wout), (targets_hbm, targets)])
    ]
    for cp in small:
        cp.start()

    peers = [along[k](d) for k in "xyz" for d in (1, 2, 3)] + [sibling] + across_x + across_z
    peers += [device(turn(e, dx), y, turn(z, dz), core) for dx in (1, 2, 3) for dz in (1, 2, 3)]
    barrier = pltpu.get_barrier_semaphore()
    for p in peers:
        pl.semaphore_signal(barrier, inc=1, device_id=p, device_id_type=MESH)

    def remote(src, dst, ss, rs, to):
        return pltpu.make_async_remote_copy(
            src_ref=src, dst_ref=dst, send_sem=ss, recv_sem=rs, device_id=to, device_id_type=MESH
        )

    leaving = {}
    turns = [0]

    def send(copies, rs, whole, sent=None):
        k = turns[0] % SENDS
        turns[0] += 1
        if k in leaving:
            leaving.pop(k)()
        ss = out_sem.at[k]
        for src, dst, to in copies:
            remote(src, dst, ss, rs, to).start()
        sent = whole if sent is None else sent
        leaving[k] = lambda: remote(sent, sent, ss, rs, sibling).wait_send()
        return lambda: remote(whole, whole, ss, rs, sibling).wait_recv()

    def spread(axis, src, dst, rs, whole, sent=None, hops=(2, 1, 3)):
        own = place[axis]
        return send([(src(turn(own, d)), dst(d, own), along[axis](d)) for d in hops], rs, whole, sent)

    def share(axis, buf, rs):
        return spread(axis, lambda k: buf.at[place[axis]], lambda d, own: buf.at[own], rs, buf.at[pl.ds(0, 3)])

    def four(ref):
        return (ref[0].astype(F32) + ref[1].astype(F32)) + (ref[2].astype(F32) + ref[3].astype(F32))

    def received(own, ref):
        total = own.astype(F32)
        for d in range(3):
            total = total + ref[d].astype(F32)
        return total

    for cp in small:
        cp.wait()
    where = lax.broadcasted_iota(jnp.int32, (8, LANES), 0) * LANES + lax.broadcasted_iota(jnp.int32, (8, LANES), 1)
    is_live = (where < live[0]).astype(F32)
    weighted_all = area[...] * is_live
    first = lax.broadcasted_iota(jnp.int32, (8, LANES), 0) == 0
    near_slot = z * 2 + core
    wt_near[near_slot] = jnp.where(
        first, jnp.sum(weighted_all, axis=0, keepdims=True), jnp.sum(is_live, axis=0, keepdims=True)
    )

    def forecast(c, m):
        f = dot(wout[...], hid[m, c * CHUNK : (c + 1) * CHUNK, :], 1, 1).astype(BF16)
        for k in range(4):
            fsend[c, k, m] = f[:, k * LANES : (k + 1) * LANES]
        frecv[c, e, m] = fsend[c, e, m]

    def forward(c, m):
        s = pl.ds(c * CHUNK, CHUNK)
        pre = jnp.dot(lat[m, s, :], w[...], preferred_element_type=F32)
        if c == 0:
            hid[m, s, :], back[m, s, :] = activation(pre)
        else:
            hid[m, s, :] = activation_only(pre)
            later[m] = pre
        forecast(c, m)

    def forward_send(c, m, hops=(2, 1, 3)):
        return spread(
            "x", lambda k: fsend.at[c, k, m], lambda d, own: frecv.at[c, own, m], f_rs.at[c, m],
            frecv.at[c, pl.ds(0, 3), m], frecv.at[c, pl.ds(0, len(hops)), m], hops,
        )

    def forward_half(c, m, hops):
        rows = [pl.ds(pl.multiple_of(c * CHUNK + turn(e, d) * LANES, LANES), LANES) for d in hops]
        pre = jnp.dot(
            jnp.concatenate([lat[m, r, :] for r in rows], axis=0), w[...], preferred_element_type=F32
        )
        h = activation_only(pre)
        for i, (r, d) in enumerate(zip(rows, hops)):
            hid[m, r, :] = h[i * LANES : (i + 1) * LANES]
            to = pl.ds(pl.multiple_of(turn(e, d) * LANES, LANES), LANES)
            later[m, to, :] = pre[i * LANES : (i + 1) * LANES]
        f = dot(wout[...], h, 1, 1).astype(BF16)
        for i, d in enumerate(hops):
            fsend[c, turn(e, d), m] = f[:, i * LANES : (i + 1) * LANES]

    def scored(c, weight_total, live_total):
        block = c * 4 + e
        y_block = targets[:, pl.ds(pl.multiple_of(block * LANES, LANES), LANES)].astype(F32)
        lanes = lax.broadcasted_iota(jnp.int32, (1, LANES), 1)
        weighted = area[pl.ds(block, 1), :] * (block * LANES + lanes < live[0]).astype(F32)
        scales = LOSS_SCALE * live_total * weighted / weight_total

        def store(m, v, step, value):
            ssend[c, m // 2, m % 2, v : v + step, :] = value

        row = score_block(frecv.at[c], y_block, weighted, scales, store)
        srecv[c, e] = ssend[c, e]
        return row

    def scored_send(c):
        return spread(
            "x", lambda k: ssend.at[c, k], lambda d, own: srecv.at[c, own], s_rs.at[c], srecv.at[c, pl.ds(0, 3)]
        )

    def backward(c, lo, wide):
        s, cols = pl.ds(c * CHUNK, CHUNK), slice(lo, lo + wide)
        for m in range(2):
            slopes = jnp.concatenate([srecv[c, k, m] for k in range(4)], axis=1)
            bh = dot(slopes, wout[:, cols], 0, 0)
            back[m, s, cols] = (back[m, s, cols].astype(F32) * bh).astype(BF16)

    def output_part(c):
        s = pl.ds(c * CHUNK, CHUNK)
        slopes = jnp.concatenate([srecv[c, k, m] for m in range(2) for k in range(4)], axis=1)
        return dot(slopes, hid[:, s, :].reshape(2 * CHUNK, FEATURES), 1, 0)

    def weight_half(c, i):
        s, cols = pl.ds(c * CHUNK, CHUNK), slice(i * HALF, (i + 1) * HALF)
        a = lat[:, s, :].reshape(2 * CHUNK, FEATURES)
        term = dot(a, back[:, s, cols].reshape(2 * CHUNK, HALF), 0, 0).reshape(16, 2, ROWS, HALF)
        if c == 0:
            acc[i] = term
        else:
            acc[i] += term

    def g_start():
        def body(k, _):
            cols = pl.ds(pl.multiple_of((k * 2 + 1 - core) * LANES, LANES), LANES)
            g_core_send[k] = gout[:, cols].astype(BF16)
            return 0

        lax.fori_loop(0, 4, body, 0)
        return send([(g_core_send, g_core_recv, sibling)], g_rs.at[0], g_core_recv)

    def g_to_first(arrived):
        arrived()

        def body(k, _):
            cols = pl.ds(pl.multiple_of((k * 2 + core) * LANES, LANES), LANES)
            g_one_send[k] = (gout[:, cols] + g_core_recv[k].astype(F32)).astype(BF16)
            return 0

        lax.fori_loop(0, 4, body, 0)
        return spread("x", lambda k: g_one_send.at[k], lambda d, own: g_one_recv.at[d - 1], g_rs.at[1], g_one_recv)

    def g_to_second(arrived):
        arrived()
        g_two[y] = received(g_one_send[e], g_one_recv).astype(BF16)
        return share("y", g_two, g_rs.at[2])

    def g_to_third(arrived):
        arrived()
        g_three[z] = four(g_two).astype(BF16)
        return share("z", g_three, g_rs.at[3])

    def g_to_all(arrived, live_total):
        arrived()
        mine = e * 2 + core
        g_all[mine] = (four(g_three) / live_total).astype(BF16)
        to = [along["x"](d) for d in (2, 1, 3)] + across_x + [sibling]
        return send([(g_all.at[mine], g_all.at[mine], p) for p in to], g_rs.at[4], g_all.at[pl.ds(0, 7)])

    def g_finish(arrived):
        arrived()
        for k in range(8):
            gwout_out[:, k * LANES : (k + 1) * LANES] = g_all[k].astype(F32)

    def to_core(i):
        core_send[i] = acc[i, :, 1 - core].astype(BF16)
        return send([(core_send.at[i], core_recv.at[i], sibling)], p_rs.at[i], core_recv.at[i])

    def from_core(i, lo, wide):
        cols = slice(lo, lo + wide)
        return (acc[i, :, core, :, cols] + core_recv[i, :, :, cols].astype(F32)).astype(BF16)

    def part(j, k):
        return one_send[j].at[k] if PIECES[j][3] == "y" else one_send[j].at[:, k]

    def to_first(j):
        half, lo, wide, axis = PIECES[j]
        one_send[j][...] = from_core(half, lo, wide).reshape(4, 4, ROWS, wide)
        return spread(
            axis, lambda k: part(j, k), lambda d, own: one_recv[j].at[d - 1], p_rs.at[2 + j], one_recv[j]
        )

    def to_second(j, arrived):
        arrived()
        axis = PIECES[j][3]
        two_send[j][...] = received(part(j, place[axis])[...], one_recv[j]).astype(BF16)
        return spread(
            "z" if axis == "y" else "y", lambda k: two_send[j].at[k], lambda d, own: two_recv[j].at[d - 1],
            p_rs.at[6 + j], two_recv[j],
        )

    def to_third(i, arrived):
        for j in (2 * i, 2 * i + 1):
            arrived[j]()
            wide, own = PIECES[j][2], place["z" if PIECES[j][3] == "y" else "y"]
            lo = (j % 2) * wide
            three[i][e, :, lo : lo + wide] = received(two_send[j][own], two_recv[j]).astype(BF16)
        return share("x", three[i], p_rs.at[10 + i])

    def finish(i, arrived, live_total):
        arrived()
        wide = 2 * PIECES[2 * i][2]
        gwin_out[:, FEATURES // 4 * (1 + i) : FEATURES // 4 * (1 + i) + wide] = four(three[i]) / live_total

    def x_block(k):
        return slice((k // 2) * 16, (k // 2 + 1) * 16), slice((k % 2) * LANES, (k % 2 + 1) * LANES)

    def x_first():
        total = from_core(0, 0, 2 * LANES)
        for k in range(4):
            rows, cols = x_block(k)
            x_send[k] = total[:, rows, cols]
        return spread("x", lambda k: x_send.at[k], lambda d, own: x_recv.at[d - 1], p_rs.at[12], x_recv)

    def x_second(arrived):
        arrived()
        xy_send[...] = received(x_send[e], x_recv).astype(BF16).reshape(4, 4, 16, LANES)
        return spread("y", lambda k: xy_send.at[k], lambda d, own: xy_recv.at[d - 1], p_rs.at[13], xy_recv)

    def x_third(arrived):
        arrived()
        xz_send[...] = received(xy_send[y], xy_recv).astype(BF16)
        slot = e * 4 + z
        x_all[slot] = xz_send[z]
        copies = []
        for dx, dz in sorted(((i, j) for i in range(4) for j in range(4) if i or j), key=lambda h: h not in FAR):
            to = turn(z, dz)
            copies.append((xz_send.at[to], x_all.at[slot], device(turn(e, dx), y, to, core)))
        return send(copies, p_rs.at[14], x_all.at[pl.ds(0, 15)])

    def x_finish(arrived, live_total):
        arrived()
        for k in range(4):
            rows, cols = x_block(k)
            gwin_out[rows, cols] = four(x_all.at[pl.ds(4 * k, 4)]) / live_total

    def latent_tile(i):
        m, s = i // 2, pl.ds((i % 2) * CHUNK, CHUNK)
        glat_out[m, s, :] = dot(back[m, s, :], w[...], 1, 1).astype(BF16)

    loads[0, 0].wait()
    load_w[0].wait()
    loads[0, 1].start()
    for i in range(2):
        cols = slice(i * HALF, (i + 1) * HALF)
        if i == 1:
            load_w[1].wait()
            loads[1, 0].start()
            loads[1, 1].start()
        pre00 = jnp.dot(lat[0, :CHUNK, :], w[:, cols], preferred_element_type=F32)
        hid[0, :CHUNK, cols], back[0, :CHUNK, cols] = activation(pre00)
    forecast(0, 0)
    pl.semaphore_wait(barrier, len(peers))
    f00 = forward_send(0, 0)
    tw = send(
        [(wt_near.at[near_slot], wt_near.at[near_slot], p) for p in [along["z"](d) for d in (2, 1, 3)] + across_z + [sibling]],
        t_rs.at[0], wt_near.at[pl.ds(0, 7)],
    )
    loads[0, 1].wait()
    forward(0, 1)
    f01 = forward_send(0, 1)
    tw()
    near = wt_near[0]
    for i in range(1, 8):
        near = near + wt_near[i]
    wt_y[y] = near
    tw = share("y", wt_y, t_rs.at[1])
    loads[1, 0].wait()
    forward(1, 0)
    f10 = forward_send(1, 0)
    loads[1, 1].wait()
    forward_half(1, 1, (2, 1))
    f11 = forward_send(1, 1, (2, 1))
    tw()
    totals = jnp.sum(four(wt_y), axis=1, keepdims=True)
    weight_total, live_total = totals[0:1, 0:1], totals[1:2, 0:1]
    f00()
    f01()
    row0 = scored(0, weight_total, live_total)
    s0 = scored_send(0)
    forward_half(1, 1, (3, 0))
    forward_send(1, 1, (3,))
    frecv[1, e, 1] = fsend[1, e, 1]
    for m in range(2):
        back[m, CHUNK:, :] = activation(later[m])[1]
    f10()
    f11()
    row1 = scored(1, weight_total, live_total)
    s1 = scored_send(1)
    ls_core[core] = jnp.broadcast_to(row0 + row1, (8, LANES))
    lc = send([(ls_core.at[core], ls_core.at[core], sibling)], t_rs.at[2], ls_core.at[0])
    s0()
    backward(0, 0, FEATURES)
    gout[...] = output_part(0)
    weight_half(0, 0)
    lc()
    ls_y[y] = ls_core[0] + ls_core[1]
    lc = share("y", ls_y, t_rs.at[3])
    weight_half(0, 1)
    s1()
    gout[...] += output_part(1)
    g = g_start()
    backward(1, 0, HALF)
    weight_half(1, 0)
    c0 = to_core(0)
    g = g_to_first(g)
    lc()
    ls_z[z] = four(ls_y)
    lc = share("z", ls_z, t_rs.at[4])
    backward(1, HALF, HALF)
    weight_half(1, 1)
    c1 = to_core(1)
    c0()
    p = {}
    xf = x_first()
    p[0] = to_first(0)
    p[1] = to_first(1)
    latent_tile(0)
    g = g_to_second(g)
    c1()
    p[2] = to_first(2)
    p[3] = to_first(3)
    latent_tile(1)
    lc()
    ls_x[e] = four(ls_z)
    lc = share("x", ls_x, t_rs.at[5])
    latent_tile(2)
    latent_tile(3)
    xf = x_second(xf)
    p[0] = to_second(0, p[0])
    p[1] = to_second(1, p[1])
    g = g_to_third(g)
    lc()
    loss_out[...] = jnp.sum(four(ls_x), axis=1, keepdims=True) / weight_total + jnp.zeros((8, LANES), F32)
    p[2] = to_second(2, p[2])
    p[3] = to_second(3, p[3])
    xf = x_third(xf)
    xa = to_third(0, p)
    g = g_to_all(g, live_total)
    xb = to_third(1, p)
    finish(0, xa, live_total)
    x_finish(xf, live_total)
    g_finish(g)
    finish(1, xb, live_total)
    for left in leaving.values():
        left()


def write_out(loss, glat, gwin, gwout, loss_out, glat_out, gwin_out, gwout_out, sem):
    pairs = [(glat, glat_out), (gwin, gwin_out), (gwout, gwout_out)]
    cps = [pltpu.make_async_copy(src, dst, sem.at[i]) for i, (src, dst) in enumerate(pairs)]
    for cp in cps:
        cp.start()
    loss_out[...] = loss[0:1, 0:1]
    for cp in cps:
        cp.wait()


def per_device(latent, w_in, output_weight, targets, area_weights, live_counts):
    vmem = pl.BlockSpec(memory_space=pltpu.VMEM)
    hbm = pl.BlockSpec(memory_space=pl.ANY)
    V = pltpu.VMEM
    dma = pltpu.SemaphoreType.DMA
    widths = [p[2] for p in PIECES]
    scratch = [
        V((2, POINTS, FEATURES), BF16),
        V((2, CHUNK, FEATURES), F32),
        V((FEATURES, FEATURES), BF16),
        V((VARS, FEATURES), BF16),
        V((VARS, POINTS), BF16),
        V((8, LANES), F32),
        V((2, POINTS, FEATURES), BF16),
        V((2, POINTS, FEATURES), BF16),
        V((2, 16, 2, ROWS, HALF), F32),
        V((CHUNKS, 4, 2, VARS, LANES), BF16),
        V((CHUNKS, 4, 2, VARS, LANES), BF16),
        V((CHUNKS, 4, 2, VARS, LANES), BF16),
        V((CHUNKS, 4, 2, VARS, LANES), BF16),
        V((VARS, FEATURES), F32),
        V((2, 16, ROWS, HALF), BF16),
        V((2, 16, ROWS, HALF), BF16),
        [V((4, 4, ROWS, n), BF16) for n in widths],
        [V((3, 4, ROWS, n), BF16) for n in widths],
        [V((4, ROWS, n), BF16) for n in widths],
        [V((3, ROWS, n), BF16) for n in widths],
        [V((4, ROWS, 2 * widths[0]), BF16), V((4, ROWS, 2 * widths[2]), BF16)],
        V((4, 16, 16, LANES), BF16),
        V((3, 16, 16, LANES), BF16),
        V((4, 4, 16, LANES), BF16),
        V((3, 4, 16, LANES), BF16),
        V((4, 16, LANES), BF16),
        V((16, 16, LANES), BF16),
        V((4, VARS, LANES), BF16),
        V((4, VARS, LANES), BF16),
        V((4, VARS, LANES), BF16),
        V((3, VARS, LANES), BF16),
        V((4, VARS, LANES), BF16),
        V((4, VARS, LANES), BF16),
        V((8, VARS, LANES), BF16),
        V((8, 8, LANES), F32),
        V((4, 8, LANES), F32),
        V((2, 8, LANES), F32),
        V((4, 8, LANES), F32),
        V((4, 8, LANES), F32),
        V((4, 8, LANES), F32),
        dma((11,)),
        dma((SENDS,)),
        dma((CHUNKS, 2)),
        dma((CHUNKS,)),
        dma((15,)),
        dma((5,)),
        dma((6,)),
    ]
    operands = (latent, w_in, output_weight, targets, area_weights.reshape(8, LANES))
    results = pl.pallas_call(
        kernel,
        out_shape=[
            V((8, LANES), F32),
            V(latent.shape, BF16),
            V((ROWS, FEATURES), F32),
            V((VARS, FEATURES), F32),
        ],
        in_specs=[pl.BlockSpec(memory_space=pltpu.HBM)] * 5 + [pl.BlockSpec(memory_space=pltpu.SMEM)],
        out_specs=[vmem] * 4,
        scratch_shapes=scratch,
        compiler_params=pltpu.CompilerParams(collective_id=1, has_side_effects=True, vmem_limit_bytes=48 << 20),
        name="energy_step",
    )(*[pltpu.with_memory_space_constraint(a, pltpu.HBM) for a in operands], live_counts)
    loss, glat, gwin, gwout = pl.pallas_call(
        write_out,
        out_shape=[
            jax.ShapeDtypeStruct((1, 1), F32),
            jax.ShapeDtypeStruct(latent.shape, BF16),
            jax.ShapeDtypeStruct((ROWS, FEATURES), F32),
            jax.ShapeDtypeStruct((VARS, FEATURES), F32),
        ],
        in_specs=[vmem] * 4,
        out_specs=[vmem] + [hbm] * 3,
        scratch_shapes=[dma((3,))],
        compiler_params=pltpu.CompilerParams(vmem_limit_bytes=1 << 20),
        name="write_out",
    )(*[pltpu.with_memory_space_constraint(r, pltpu.VMEM) for r in results])
    return loss.reshape(()), glat, gwin, gwout


def solution(mesh):
    placed = (P("ens", "sp", None), P(), P(), P(None, "sp"), P("sp"), P("sp"))
    return jax.shard_map(
        per_device,
        mesh=mesh,
        in_specs=placed,
        out_specs=(P(), P("ens", "sp", None), P("sp", None), P()),
        check_vma=False,
    )
```

time: 54.4 us -> 51 us (0.938)
  Pallas kernels: 52.8 us -> 49.4 us
    pallas_call x1, Pallas kernels: 50 us -> 46.8 us  [per_device(): pl.pallas_call(kernel, out_shape=[V((8, LANES), F32), V(latent.shape, BF1...]
where the time goes in v3:
time: 51 us; the launch traced here: 50.9 us
  Pallas kernels  49.4 us (97%)
  between operations  1.45 us (3%)
    pallas_call x1, Pallas kernels, per_device(): pl.pallas_call(kernel, out_shape=[V((8, LANES), F32), V(latent.shape, BF1...  46.8 us
    pallas_call x1, Pallas kernels, per_device(): pl.pallas_call(write_out, out_shape=[jax.ShapeDtypeStruct((1, 1), F32), j...  2.68 us

profile of v3, /device:TPU:1, one launch (start us, length us, event | category | flops | bytes accessed | tf_op | source)
XLA Modules:
  0.0 50.9 jit_solution(17638218607143563579)
XLA Ops:
  1.3 46.8 %energy_step.1 = (f32[8,128]{1,0:T(8,128)S(1)}, bf16[2,1024,1024]{2,1,0:T(8,128)(2,1)S(1)}, f32[32,1024]{1,0:T(8,128)S(1)}, f32[80,1024]{1,0:T(8,128)S(1)}) custom-call(bf16[2,1024,1024]{2,1,0:T(8,128)(2,1)} %lat_hbm.1, bf16[1024,1024]{1,0:T(8,128)(2,1)} %w_hbm.1, bf16[80,1024]{1,0:T(8,128)(2,1)} %wout_hbm.1, bf16[80,1024]{1,0:T(8,128)(2,1)} %targets_hbm.1, ...), custom_call_target="tpu_custom_call" | custom-call | tf_op jit(solution)/shard_map/energy_step/pallas_call | solution.py:545
  48.1 2.7 %write_out.1 = (f32[1,1]{1,0:T(1,128)}, bf16[2,1024,1024]{2,1,0:T(8,128)(2,1)}, f32[32,1024]{1,0:T(8,128)}, f32[80,1024]{1,0:T(8,128)}) custom-call(f32[8,128]{1,0:T(8,128)S(1)} %get-tuple-element.12.loss, bf16[2,1024,1024]{2,1,0:T(8,128)(2,1)S(1)} %get-tuple-element.13.glat, f32[32,1024]{1,0:T(8,128)S(1)} %get-tuple-element.14.gwin, ...), custom_call_target="tpu_custom_call" | custom-call | tf_op jit(solution)/shard_map/write_out/pallas_call | solution.py:559

commit v4 on v3

--- a/solution.py
+++ b/solution.py
@@ -40,7 +40,7 @@
     return (z * (0.5 * jnp.tanh(z * (INNER * (z * z) + OUTER)) + 0.5)).astype(BF16)
 
 
-def score_block(x_ref, y, weighted, scales, store):
+def score_block(x_ref, y, weighted, store):
     n = MEMBERS
     pairs = [(i, j) for i in range(n) for j in range(i + 1, n)]
     step = 16
@@ -57,8 +57,8 @@
     a = [jnp.sqrt(jnp.sum(o, axis=0, keepdims=True) + 1.0) for o in own]
     b = [jnp.sqrt(jnp.sum(o, axis=0, keepdims=True) + 1.0) for o in between]
     score = sum(a) / n - sum(b) / (n * (n - 1.0))
-    from_target = [scales / (n * t) for t in a]
-    from_pair = [scales / (n * (n - 1.0) * t) for t in b]
+    from_target = [weighted / (n * t) for t in a]
+    from_pair = [weighted / (n * (n - 1.0) * t) for t in b]
     for v in range(0, VARS, step):
         x = [x_ref[m // 2, m % 2, v : v + step, :].astype(F32) for m in range(n)]
         total = [(x[m] - y[v : v + step]) * from_target[m] for m in range(n)]
@@ -78,7 +78,7 @@
     core_send, core_recv, one_send, one_recv, two_send, two_recv, three,
     x_send, x_recv, xy_send, xy_recv, xz_send, x_all,
     g_core_send, g_core_recv, g_one_send, g_one_recv, g_two, g_three, g_all,
-    wt_near, wt_y, ls_core, ls_y, ls_z, ls_x,
+    ls_core, ls_y, ls_z, ls_x,
     in_sem, out_sem, f_rs, s_rs, p_rs, g_rs, t_rs,
 ):
     e = lax.axis_index("ens")
@@ -100,28 +100,26 @@
     }
     place = {"x": e, "y": y, "z": z}
     sibling = device(e, y, z, 1 - core)
-    across_x = [device(turn(e, d), y, z, 1 - core) for d in (1, 2, 3)]
-    across_z = [device(e, y, turn(z, d), 1 - core) for d in (1, 2, 3)]
 
     def load(m, c):
         s = pl.ds(c * CHUNK, CHUNK)
         return pltpu.make_async_copy(lat_hbm.at[m, s], lat.at[m, s], in_sem.at[2 * c + m])
 
     loads = {(c, m): load(m, c) for c in range(CHUNKS) for m in range(2)}
+    small = [
+        pltpu.make_async_copy(src, dst, in_sem.at[8 + i])
+        for i, (src, dst) in enumerate([(area_hbm, area), (wout_hbm, wout), (targets_hbm, targets)])
+    ]
     loads[0, 0].start()
     load_w = []
     for i in range(2):
         cols = pl.ds(i * HALF, HALF)
         load_w.append(pltpu.make_async_copy(w_hbm.at[:, cols], w.at[:, cols], in_sem.at[4 + i]))
         load_w[i].start()
-    small = [
-        pltpu.make_async_copy(src, dst, in_sem.at[8 + i])
-        for i, (src, dst) in enumerate([(area_hbm, area), (wout_hbm, wout), (targets_hbm, targets)])
-    ]
     for cp in small:
         cp.start()
 
-    peers = [along[k](d) for k in "xyz" for d in (1, 2, 3)] + [sibling] + across_x + across_z
+    peers = [along[k](d) for k in "xyz" for d in (1, 2, 3)] + [sibling]
     peers += [device(turn(e, dx), y, turn(z, dz), core) for dx in (1, 2, 3) for dz in (1, 2, 3)]
     barrier = pltpu.get_barrier_semaphore()
     for p in peers:
@@ -163,16 +161,16 @@
             total = total + ref[d].astype(F32)
         return total
 
-    for cp in small:
-        cp.wait()
-    where = lax.broadcasted_iota(jnp.int32, (8, LANES), 0) * LANES + lax.broadcasted_iota(jnp.int32, (8, LANES), 1)
-    is_live = (where < live[0]).astype(F32)
-    weighted_all = area[...] * is_live
-    first = lax.broadcasted_iota(jnp.int32, (8, LANES), 0) == 0
-    near_slot = z * 2 + core
-    wt_near[near_slot] = jnp.where(
-        first, jnp.sum(weighted_all, axis=0, keepdims=True), jnp.sum(is_live, axis=0, keepdims=True)
-    )
+    def sums_tile(scores):
+        where = lax.broadcasted_iota(jnp.int32, (8, LANES), 0) * LANES + lax.broadcasted_iota(jnp.int32, (8, LANES), 1)
+        is_live = (where < live[0]).astype(F32)
+        row = lax.broadcasted_iota(jnp.int32, (8, LANES), 0)
+        weights = jnp.sum(area[...] * is_live, axis=0, keepdims=True)
+        return jnp.where(row == 0, scores, jnp.where(row == 1, weights, jnp.sum(is_live, axis=0, keepdims=True)))
+
+    def slopes_of_gelu(c, m):
+        s = pl.ds(c * CHUNK, CHUNK)
+        back[m, s, :] = activation(later[m, s, :])[1]
 
     def forecast(c, m):
         f = dot(wout[...], hid[m, c * CHUNK : (c + 1) * CHUNK, :], 1, 1).astype(BF16)
@@ -183,11 +181,8 @@
     def forward(c, m):
         s = pl.ds(c * CHUNK, CHUNK)
         pre = jnp.dot(lat[m, s, :], w[...], preferred_element_type=F32)
-        if c == 0:
-            hid[m, s, :], back[m, s, :] = activation(pre)
-        else:
-            hid[m, s, :] = activation_only(pre)
-            later[m] = pre
+        hid[m, s, :] = activation_only(pre)
+        later[m, s, :] = pre
         forecast(c, m)
 
     def forward_send(c, m, hops=(2, 1, 3)):
@@ -202,25 +197,23 @@
             jnp.concatenate([lat[m, r, :] for r in rows], axis=0), w[...], preferred_element_type=F32
         )
         h = activation_only(pre)
-        for i, (r, d) in enumerate(zip(rows, hops)):
+        for i, r in enumerate(rows):
             hid[m, r, :] = h[i * LANES : (i + 1) * LANES]
-            to = pl.ds(pl.multiple_of(turn(e, d) * LANES, LANES), LANES)
-            later[m, to, :] = pre[i * LANES : (i + 1) * LANES]
+            later[m, r, :] = pre[i * LANES : (i + 1) * LANES]
         f = dot(wout[...], h, 1, 1).astype(BF16)
         for i, d in enumerate(hops):
             fsend[c, turn(e, d), m] = f[:, i * LANES : (i + 1) * LANES]
 
-    def scored(c, weight_total, live_total):
+    def scored(c):
         block = c * 4 + e
         y_block = targets[:, pl.ds(pl.multiple_of(block * LANES, LANES), LANES)].astype(F32)
         lanes = lax.broadcasted_iota(jnp.int32, (1, LANES), 1)
         weighted = area[pl.ds(block, 1), :] * (block * LANES + lanes < live[0]).astype(F32)
-        scales = LOSS_SCALE * live_total * weighted / weight_total
 
         def store(m, v, step, value):
             ssend[c, m // 2, m % 2, v : v + step, :] = value
 
-        row = score_block(frecv.at[c], y_block, weighted, scales, store)
+        row = score_block(frecv.at[c], y_block, weighted, store)
         srecv[c, e] = ssend[c, e]
         return row
 
@@ -241,14 +234,16 @@
         slopes = jnp.concatenate([srecv[c, k, m] for m in range(2) for k in range(4)], axis=1)
         return dot(slopes, hid[:, s, :].reshape(2 * CHUNK, FEATURES), 1, 0)
 
-    def weight_half(c, i):
-        s, cols = pl.ds(c * CHUNK, CHUNK), slice(i * HALF, (i + 1) * HALF)
-        a = lat[:, s, :].reshape(2 * CHUNK, FEATURES)
-        term = dot(a, back[:, s, cols].reshape(2 * CHUNK, HALF), 0, 0).reshape(16, 2, ROWS, HALF)
-        if c == 0:
-            acc[i] = term
-        else:
-            acc[i] += term
+    def weight_early():
+        a = lat[:, :CHUNK, :].reshape(2 * CHUNK, FEATURES)
+        term = dot(a, back[:, :CHUNK, :].reshape(2 * CHUNK, FEATURES), 0, 0)
+        for i in range(2):
+            acc[i] = term[:, i * HALF : (i + 1) * HALF].reshape(16, 2, ROWS, HALF)
+
+    def weight_half(i):
+        cols = slice(i * HALF, (i + 1) * HALF)
+        a = lat[:, CHUNK:, :].reshape(2 * CHUNK, FEATURES)
+        acc[i] += dot(a, back[:, CHUNK:, cols].reshape(2 * CHUNK, HALF), 0, 0).reshape(16, 2, ROWS, HALF)
 
     def g_start():
         def body(k, _):
@@ -268,29 +263,31 @@
             return 0
 
         lax.fori_loop(0, 4, body, 0)
-        return spread("x", lambda k: g_one_send.at[k], lambda d, own: g_one_recv.at[d - 1], g_rs.at[1], g_one_recv)
+        return spread("y", lambda k: g_one_send.at[k], lambda d, own: g_one_recv.at[d - 1], g_rs.at[1], g_one_recv)
 
     def g_to_second(arrived):
         arrived()
-        g_two[y] = received(g_one_send[e], g_one_recv).astype(BF16)
-        return share("y", g_two, g_rs.at[2])
+        g_two[e] = received(g_one_send[y], g_one_recv).astype(BF16)
+        return share("x", g_two, g_rs.at[2])
 
     def g_to_third(arrived):
         arrived()
         g_three[z] = four(g_two).astype(BF16)
         return share("z", g_three, g_rs.at[3])
 
-    def g_to_all(arrived, live_total):
-        arrived()
-        mine = e * 2 + core
-        g_all[mine] = (four(g_three) / live_total).astype(BF16)
-        to = [along["x"](d) for d in (2, 1, 3)] + across_x + [sibling]
-        return send([(g_all.at[mine], g_all.at[mine], p) for p in to], g_rs.at[4], g_all.at[pl.ds(0, 7)])
+    def g_to_all(arrived, share_of):
+        arrived()
+        g_all[core, y] = (four(g_three) * share_of).astype(BF16)
+        return spread("y", lambda k: g_all.at[core, y], lambda d, own: g_all.at[core, own], g_rs.at[4], g_all.at[0, pl.ds(0, 3)])
+
+    def g_to_sibling(arrived):
+        arrived()
+        return send([(g_all.at[core], g_all.at[core], sibling)], g_rs.at[5], g_all.at[0])
 
     def g_finish(arrived):
         arrived()
         for k in range(8):
-            gwout_out[:, k * LANES : (k + 1) * LANES] = g_all[k].astype(F32)
+            gwout_out[:, k * LANES : (k + 1) * LANES] = g_all[k % 2, k // 2].astype(F32)
 
     def to_core(i):
         core_send[i] = acc[i, :, 1 - core].astype(BF16)
@@ -327,10 +324,10 @@
             three[i][e, :, lo : lo + wide] = received(two_send[j][own], two_recv[j]).astype(BF16)
         return share("x", three[i], p_rs.at[10 + i])
 
-    def finish(i, arrived, live_total):
+    def finish(i, arrived, share_of):
         arrived()
         wide = 2 * PIECES[2 * i][2]
-        gwin_out[:, FEATURES // 4 * (1 + i) : FEATURES // 4 * (1 + i) + wide] = four(three[i]) / live_total
+        gwin_out[:, FEATURES // 4 * (1 + i) : FEATURES // 4 * (1 + i) + wide] = four(three[i]) * share_of
 
     def x_block(k):
         return slice((k // 2) * 16, (k // 2 + 1) * 16), slice((k % 2) * LANES, (k % 2 + 1) * LANES)
@@ -358,15 +355,15 @@
             copies.append((xz_send.at[to], x_all.at[slot], device(turn(e, dx), y, to, core)))
         return send(copies, p_rs.at[14], x_all.at[pl.ds(0, 15)])
 
-    def x_finish(arrived, live_total):
+    def x_finish(arrived, share_of):
         arrived()
         for k in range(4):
             rows, cols = x_block(k)
-            gwin_out[rows, cols] = four(x_all.at[pl.ds(4 * k, 4)]) / live_total
-
-    def latent_tile(i):
+            gwin_out[rows, cols] = four(x_all.at[pl.ds(4 * k, 4)]) * share_of
+
+    def latent_tile(i, factor):
         m, s = i // 2, pl.ds((i % 2) * CHUNK, CHUNK)
-        glat_out[m, s, :] = dot(back[m, s, :], w[...], 1, 1).astype(BF16)
+        glat_out[m, s, :] = (dot(back[m, s, :], w[...], 1, 1) * factor).astype(BF16)
 
     loads[0, 0].wait()
     load_w[0].wait()
@@ -379,99 +376,95 @@
             loads[1, 1].start()
         pre00 = jnp.dot(lat[0, :CHUNK, :], w[:, cols], preferred_element_type=F32)
         hid[0, :CHUNK, cols], back[0, :CHUNK, cols] = activation(pre00)
+    small[1].wait()
     forecast(0, 0)
     pl.semaphore_wait(barrier, len(peers))
     f00 = forward_send(0, 0)
-    tw = send(
-        [(wt_near.at[near_slot], wt_near.at[near_slot], p) for p in [along["z"](d) for d in (2, 1, 3)] + across_z + [sibling]],
-        t_rs.at[0], wt_near.at[pl.ds(0, 7)],
-    )
     loads[0, 1].wait()
     forward(0, 1)
     f01 = forward_send(0, 1)
-    tw()
-    near = wt_near[0]
-    for i in range(1, 8):
-        near = near + wt_near[i]
-    wt_y[y] = near
-    tw = share("y", wt_y, t_rs.at[1])
     loads[1, 0].wait()
     forward(1, 0)
     f10 = forward_send(1, 0)
     loads[1, 1].wait()
     forward_half(1, 1, (2, 1))
     f11 = forward_send(1, 1, (2, 1))
-    tw()
-    totals = jnp.sum(four(wt_y), axis=1, keepdims=True)
-    weight_total, live_total = totals[0:1, 0:1], totals[1:2, 0:1]
     f00()
     f01()
-    row0 = scored(0, weight_total, live_total)
+    small[0].wait()
+    small[2].wait()
+    row0 = scored(0)
     s0 = scored_send(0)
     forward_half(1, 1, (3, 0))
     forward_send(1, 1, (3,))
     frecv[1, e, 1] = fsend[1, e, 1]
-    for m in range(2):
-        back[m, CHUNK:, :] = activation(later[m])[1]
+    slopes_of_gelu(0, 1)
+    slopes_of_gelu(1, 0)
+    slopes_of_gelu(1, 1)
     f10()
     f11()
-    row1 = scored(1, weight_total, live_total)
+    row1 = scored(1)
     s1 = scored_send(1)
-    ls_core[core] = jnp.broadcast_to(row0 + row1, (8, LANES))
-    lc = send([(ls_core.at[core], ls_core.at[core], sibling)], t_rs.at[2], ls_core.at[0])
+    ls_core[core] = sums_tile(row0 + row1)
+    lc = send([(ls_core.at[core], ls_core.at[core], sibling)], t_rs.at[0], ls_core.at[0])
     s0()
     backward(0, 0, FEATURES)
     gout[...] = output_part(0)
-    weight_half(0, 0)
     lc()
     ls_y[y] = ls_core[0] + ls_core[1]
-    lc = share("y", ls_y, t_rs.at[3])
-    weight_half(0, 1)
+    lc = share("y", ls_y, t_rs.at[1])
+    weight_early()
     s1()
     gout[...] += output_part(1)
     g = g_start()
+    lc()
+    ls_z[z] = four(ls_y)
+    lc = share("z", ls_z, t_rs.at[2])
     backward(1, 0, HALF)
-    weight_half(1, 0)
+    weight_half(0)
     c0 = to_core(0)
     g = g_to_first(g)
-    lc()
-    ls_z[z] = four(ls_y)
-    lc = share("z", ls_z, t_rs.at[4])
     backward(1, HALF, HALF)
-    weight_half(1, 1)
+    weight_half(1)
     c1 = to_core(1)
     c0()
     p = {}
     xf = x_first()
     p[0] = to_first(0)
     p[1] = to_first(1)
-    latent_tile(0)
+    lc()
+    sums = four(ls_z)
+    ls_x[e] = sums
+    lc = share("x", ls_x, t_rs.at[3])
+    totals = jnp.sum(sums, axis=1, keepdims=True)
+    weight_total, live_total = totals[1:2, 0:1], totals[2:3, 0:1]
+    factor = LOSS_SCALE * live_total / weight_total
+    latent_tile(0, factor)
     g = g_to_second(g)
     c1()
     p[2] = to_first(2)
     p[3] = to_first(3)
-    latent_tile(1)
-    lc()
-    ls_x[e] = four(ls_z)
-    lc = share("x", ls_x, t_rs.at[5])
-    latent_tile(2)
-    latent_tile(3)
+    latent_tile(1, factor)
+    latent_tile(2, factor)
     xf = x_second(xf)
     p[0] = to_second(0, p[0])
     p[1] = to_second(1, p[1])
     g = g_to_third(g)
+    latent_tile(3, factor)
     lc()
     loss_out[...] = jnp.sum(four(ls_x), axis=1, keepdims=True) / weight_total + jnp.zeros((8, LANES), F32)
+    share_of = LOSS_SCALE / weight_total
     p[2] = to_second(2, p[2])
     p[3] = to_second(3, p[3])
     xf = x_third(xf)
     xa = to_third(0, p)
-    g = g_to_all(g, live_total)
+    g = g_to_all(g, share_of)
     xb = to_third(1, p)
-    finish(0, xa, live_total)
-    x_finish(xf, live_total)
+    finish(0, xa, share_of)
+    g = g_to_sibling(g)
+    x_finish(xf, share_of)
     g_finish(g)
-    finish(1, xb, live_total)
+    finish(1, xb, share_of)
     for left in leaving.values():
         left()
 
@@ -494,7 +487,7 @@
     widths = [p[2] for p in PIECES]
     scratch = [
         V((2, POINTS, FEATURES), BF16),
-        V((2, CHUNK, FEATURES), F32),
+        V((2, POINTS, FEATURES), F32),
         V((FEATURES, FEATURES), BF16),
         V((VARS, FEATURES), BF16),
         V((VARS, POINTS), BF16),
@@ -526,9 +519,7 @@
         V((3, VARS, LANES), BF16),
         V((4, VARS, LANES), BF16),
         V((4, VARS, LANES), BF16),
-        V((8, VARS, LANES), BF16),
-        V((8, 8, LANES), F32),
-        V((4, 8, LANES), F32),
+        V((2, 4, VARS, LANES), BF16),
         V((2, 8, LANES), F32),
         V((4, 8, LANES), F32),
         V((4, 8, LANES), F32),
@@ -538,8 +529,8 @@
         dma((CHUNKS, 2)),
         dma((CHUNKS,)),
         dma((15,)),
-        dma((5,)),
         dma((6,)),
+        dma((4,)),
     ]
     operands = (latent, w_in, output_weight, targets, area_weights.reshape(8, LANES))
     results = pl.pallas_call(

time: 51 us -> 51.9 us (1.018)
  Pallas kernels: 49.4 us -> 50.4 us
    pallas_call x1, Pallas kernels: 46.8 us -> 47.7 us  [per_device(): pl.pallas_call(kernel, out_shape=[V((8, LANES), F32), V(latent.shape, BF1...]
where the time goes in v4:
time: 51.9 us; the launch traced here: 51.8 us
  Pallas kernels  50.4 us (97%)
  between operations  1.45 us (3%)
    pallas_call x1, Pallas kernels, per_device(): pl.pallas_call(kernel, out_shape=[V((8, LANES), F32), V(latent.shape, BF1...  47.7 us
    pallas_call x1, Pallas kernels, per_device(): pl.pallas_call(write_out, out_shape=[jax.ShapeDtypeStruct((1, 1), F32), j...  2.68 us

profile of v4, /device:TPU:1, one launch (start us, length us, event | category | flops | bytes accessed | tf_op | source)
XLA Modules:
  0.0 51.8 jit_solution(14398483053872950251)
XLA Ops:
  1.3 47.7 %energy_step.1 = (f32[8,128]{1,0:T(8,128)S(1)}, bf16[2,1024,1024]{2,1,0:T(8,128)(2,1)S(1)}, f32[32,1024]{1,0:T(8,128)S(1)}, f32[80,1024]{1,0:T(8,128)S(1)}) custom-call(bf16[2,1024,1024]{2,1,0:T(8,128)(2,1)} %lat_hbm.1, bf16[1024,1024]{1,0:T(8,128)(2,1)} %w_hbm.1, bf16[80,1024]{1,0:T(8,128)(2,1)} %wout_hbm.1, bf16[80,1024]{1,0:T(8,128)(2,1)} %targets_hbm.1, ...), custom_call_target="tpu_custom_call" | custom-call | tf_op jit(solution)/shard_map/energy_step/pallas_call | solution.py:536
  49.0 2.7 %write_out.1 = (f32[1,1]{1,0:T(1,128)}, bf16[2,1024,1024]{2,1,0:T(8,128)(2,1)}, f32[32,1024]{1,0:T(8,128)}, f32[80,1024]{1,0:T(8,128)}) custom-call(f32[8,128]{1,0:T(8,128)S(1)} %get-tuple-element.12.loss, bf16[2,1024,1024]{2,1,0:T(8,128)(2,1)S(1)} %get-tuple-element.13.glat, f32[32,1024]{1,0:T(8,128)S(1)} %get-tuple-element.14.gwin, ...), custom_call_target="tpu_custom_call" | custom-call | tf_op jit(solution)/shard_map/write_out/pallas_call | solution.py:550

commit v5 on v4

--- a/solution.py
+++ b/solution.py
@@ -185,6 +185,10 @@
         later[m, s, :] = pre
         forecast(c, m)
 
+    def forward_first(cols):
+        pre = jnp.dot(lat[0, :CHUNK, :], w[:, cols], preferred_element_type=F32)
+        hid[0, :CHUNK, cols], back[0, :CHUNK, cols] = activation(pre)
+
     def forward_send(c, m, hops=(2, 1, 3)):
         return spread(
             "x", lambda k: fsend.at[c, k, m], lambda d, own: frecv.at[c, own, m], f_rs.at[c, m],
@@ -232,7 +236,11 @@
     def output_part(c):
         s = pl.ds(c * CHUNK, CHUNK)
         slopes = jnp.concatenate([srecv[c, k, m] for m in range(2) for k in range(4)], axis=1)
-        return dot(slopes, hid[:, s, :].reshape(2 * CHUNK, FEATURES), 1, 0)
+        term = dot(slopes, hid[:, s, :].reshape(2 * CHUNK, FEATURES), 1, 0)
+        if c == 0:
+            gout[...] = term
+        else:
+            gout[...] += term
 
     def weight_early():
         a = lat[:, :CHUNK, :].reshape(2 * CHUNK, FEATURES)
@@ -364,6 +372,9 @@
     def latent_tile(i, factor):
         m, s = i // 2, pl.ds((i % 2) * CHUNK, CHUNK)
         glat_out[m, s, :] = (dot(back[m, s, :], w[...], 1, 1) * factor).astype(BF16)
+
+    def block(run, *args):
+        pl.when(core < 2)(lambda: run(*args))
 
     loads[0, 0].wait()
     load_w[0].wait()
@@ -374,20 +385,19 @@
             load_w[1].wait()
             loads[1, 0].start()
             loads[1, 1].start()
-        pre00 = jnp.dot(lat[0, :CHUNK, :], w[:, cols], preferred_element_type=F32)
-        hid[0, :CHUNK, cols], back[0, :CHUNK, cols] = activation(pre00)
+        block(forward_first, cols)
     small[1].wait()
-    forecast(0, 0)
+    block(forecast, 0, 0)
     pl.semaphore_wait(barrier, len(peers))
     f00 = forward_send(0, 0)
     loads[0, 1].wait()
-    forward(0, 1)
+    block(forward, 0, 1)
     f01 = forward_send(0, 1)
     loads[1, 0].wait()
-    forward(1, 0)
+    block(forward, 1, 0)
     f10 = forward_send(1, 0)
     loads[1, 1].wait()
-    forward_half(1, 1, (2, 1))
+    block(forward_half, 1, 1, (2, 1))
     f11 = forward_send(1, 1, (2, 1))
     f00()
     f01()
@@ -395,12 +405,12 @@
     small[2].wait()
     row0 = scored(0)
     s0 = scored_send(0)
-    forward_half(1, 1, (3, 0))
+    block(forward_half, 1, 1, (3, 0))
     forward_send(1, 1, (3,))
     frecv[1, e, 1] = fsend[1, e, 1]
-    slopes_of_gelu(0, 1)
-    slopes_of_gelu(1, 0)
-    slopes_of_gelu(1, 1)
+    block(slopes_of_gelu, 0, 1)
+    block(slopes_of_gelu, 1, 0)
+    block(slopes_of_gelu, 1, 1)
     f10()
     f11()
     row1 = scored(1)
@@ -408,24 +418,24 @@
     ls_core[core] = sums_tile(row0 + row1)
     lc = send([(ls_core.at[core], ls_core.at[core], sibling)], t_rs.at[0], ls_core.at[0])
     s0()
-    backward(0, 0, FEATURES)
-    gout[...] = output_part(0)
+    block(backward, 0, 0, FEATURES)
+    block(output_part, 0)
     lc()
     ls_y[y] = ls_core[0] + ls_core[1]
     lc = share("y", ls_y, t_rs.at[1])
-    weight_early()
+    block(weight_early)
     s1()
-    gout[...] += output_part(1)
+    block(output_part, 1)
     g = g_start()
     lc()
     ls_z[z] = four(ls_y)
     lc = share("z", ls_z, t_rs.at[2])
-    backward(1, 0, HALF)
-    weight_half(0)
+    block(backward, 1, 0, HALF)
+    block(weight_half, 0)
     c0 = to_core(0)
     g = g_to_first(g)
-    backward(1, HALF, HALF)
-    weight_half(1)
+    block(backward, 1, HALF, HALF)
+    block(weight_half, 1)
     c1 = to_core(1)
     c0()
     p = {}
@@ -439,18 +449,18 @@
     totals = jnp.sum(sums, axis=1, keepdims=True)
     weight_total, live_total = totals[1:2, 0:1], totals[2:3, 0:1]
     factor = LOSS_SCALE * live_total / weight_total
-    latent_tile(0, factor)
+    block(latent_tile, 0, factor)
     g = g_to_second(g)
     c1()
     p[2] = to_first(2)
     p[3] = to_first(3)
-    latent_tile(1, factor)
-    latent_tile(2, factor)
+    block(latent_tile, 1, factor)
+    block(latent_tile, 2, factor)
     xf = x_second(xf)
     p[0] = to_second(0, p[0])
     p[1] = to_second(1, p[1])
     g = g_to_third(g)
-    latent_tile(3, factor)
+    block(latent_tile, 3, factor)
     lc()
     loss_out[...] = jnp.sum(four(ls_x), axis=1, keepdims=True) / weight_total + jnp.zeros((8, LANES), F32)
     share_of = LOSS_SCALE / weight_total

time: 51.9 us -> 48.6 us (0.936)
  Pallas kernels: 50.4 us -> 47.1 us
    pallas_call x1, Pallas kernels: 47.7 us -> 44.4 us  [per_device(): pl.pallas_call(kernel, out_shape=[V((8, LANES), F32), V(latent.shape, BF1...]
where the time goes in v5:
time: 48.6 us; the launch traced here: 48.5 us
  Pallas kernels  47.1 us (97%)
  between operations  1.45 us (3%)
    pallas_call x1, Pallas kernels, per_device(): pl.pallas_call(kernel, out_shape=[V((8, LANES), F32), V(latent.shape, BF1...  44.4 us
    pallas_call x1, Pallas kernels, per_device(): pl.pallas_call(write_out, out_shape=[jax.ShapeDtypeStruct((1, 1), F32), j...  2.68 us

profile of v5, /device:TPU:1, one launch (start us, length us, event | category | flops | bytes accessed | tf_op | source)
XLA Modules:
  0.0 48.5 jit_solution(12608974691932710853)
XLA Ops:
  1.3 44.4 %energy_step.1 = (f32[8,128]{1,0:T(8,128)S(1)}, bf16[2,1024,1024]{2,1,0:T(8,128)(2,1)S(1)}, f32[32,1024]{1,0:T(8,128)S(1)}, f32[80,1024]{1,0:T(8,128)S(1)}) custom-call(bf16[2,1024,1024]{2,1,0:T(8,128)(2,1)} %lat_hbm.1, bf16[1024,1024]{1,0:T(8,128)(2,1)} %w_hbm.1, bf16[80,1024]{1,0:T(8,128)(2,1)} %wout_hbm.1, bf16[80,1024]{1,0:T(8,128)(2,1)} %targets_hbm.1, ...), custom_call_target="tpu_custom_call" | custom-call | tf_op jit(solution)/shard_map/energy_step/pallas_call | solution.py:546
  45.7 2.7 %write_out.1 = (f32[1,1]{1,0:T(1,128)}, bf16[2,1024,1024]{2,1,0:T(8,128)(2,1)}, f32[32,1024]{1,0:T(8,128)}, f32[80,1024]{1,0:T(8,128)}) custom-call(f32[8,128]{1,0:T(8,128)S(1)} %get-tuple-element.12.loss, bf16[2,1024,1024]{2,1,0:T(8,128)(2,1)S(1)} %get-tuple-element.13.glat, f32[32,1024]{1,0:T(8,128)S(1)} %get-tuple-element.14.gwin, ...), custom_call_target="tpu_custom_call" | custom-call | tf_op jit(solution)/shard_map/write_out/pallas_call | solution.py:560

commit v6 on v5

--- a/solution.py
+++ b/solution.py
@@ -449,11 +449,11 @@
     totals = jnp.sum(sums, axis=1, keepdims=True)
     weight_total, live_total = totals[1:2, 0:1], totals[2:3, 0:1]
     factor = LOSS_SCALE * live_total / weight_total
-    block(latent_tile, 0, factor)
-    g = g_to_second(g)
     c1()
     p[2] = to_first(2)
     p[3] = to_first(3)
+    block(latent_tile, 0, factor)
+    g = g_to_second(g)
     block(latent_tile, 1, factor)
     block(latent_tile, 2, factor)
     xf = x_second(xf)

time: 48.6 us -> 48.4 us (level)
  no operation moved by 1% of the time
where the time goes in v6:
time: 48.4 us; the launch traced here: 48.2 us
  Pallas kernels  46.8 us (97%)
  between operations  1.45 us (3%)
    pallas_call x1, Pallas kernels, per_device(): pl.pallas_call(kernel, out_shape=[V((8, LANES), F32), V(latent.shape, BF1...  44.1 us
    pallas_call x1, Pallas kernels, per_device(): pl.pallas_call(write_out, out_shape=[jax.ShapeDtypeStruct((1, 1), F32), j...  2.68 us

profile of v6, /device:TPU:1, one launch (start us, length us, event | category | flops | bytes accessed | tf_op | source)
XLA Modules:
  0.0 48.2 jit_solution(8144863217261687461)
XLA Ops:
  1.3 44.1 %energy_step.1 = (f32[8,128]{1,0:T(8,128)S(1)}, bf16[2,1024,1024]{2,1,0:T(8,128)(2,1)S(1)}, f32[32,1024]{1,0:T(8,128)S(1)}, f32[80,1024]{1,0:T(8,128)S(1)}) custom-call(bf16[2,1024,1024]{2,1,0:T(8,128)(2,1)} %lat_hbm.1, bf16[1024,1024]{1,0:T(8,128)(2,1)} %w_hbm.1, bf16[80,1024]{1,0:T(8,128)(2,1)} %wout_hbm.1, bf16[80,1024]{1,0:T(8,128)(2,1)} %targets_hbm.1, ...), custom_call_target="tpu_custom_call" | custom-call | tf_op jit(solution)/shard_map/energy_step/pallas_call | solution.py:546
  45.4 2.7 %write_out.1 = (f32[1,1]{1,0:T(1,128)}, bf16[2,1024,1024]{2,1,0:T(8,128)(2,1)}, f32[32,1024]{1,0:T(8,128)}, f32[80,1024]{1,0:T(8,128)}) custom-call(f32[8,128]{1,0:T(8,128)S(1)} %get-tuple-element.12.loss, bf16[2,1024,1024]{2,1,0:T(8,128)(2,1)S(1)} %get-tuple-element.13.glat, f32[32,1024]{1,0:T(8,128)S(1)} %get-tuple-element.14.gwin, ...), custom_call_target="tpu_custom_call" | custom-call | tf_op jit(solution)/shard_map/write_out/pallas_call | solution.py:560

commit v7 on v6

--- a/solution.py
+++ b/solution.py
@@ -30,9 +30,9 @@
 
 def activation(z):
     cubic = INNER * (z * z)
-    s = 0.5 * jnp.tanh(z * (cubic + OUTER)) + 0.5
-    h = z * s
-    slope = s + (h - h * s) * (6.0 * cubic + 2.0 * OUTER)
+    t = jnp.tanh(z * (cubic + OUTER))
+    h = z * (0.5 * t + 0.5)
+    slope = (1.0 + t) * (1.0 + (1.0 - t) * (z * (3.0 * cubic + OUTER)))
     return h.astype(BF16), slope.astype(BF16)
 
 
@@ -448,7 +448,7 @@
     lc = share("x", ls_x, t_rs.at[3])
     totals = jnp.sum(sums, axis=1, keepdims=True)
     weight_total, live_total = totals[1:2, 0:1], totals[2:3, 0:1]
-    factor = LOSS_SCALE * live_total / weight_total
+    factor = 0.5 * LOSS_SCALE * live_total / weight_total
     c1()
     p[2] = to_first(2)
     p[3] = to_first(3)
@@ -464,17 +464,18 @@
     lc()
     loss_out[...] = jnp.sum(four(ls_x), axis=1, keepdims=True) / weight_total + jnp.zeros((8, LANES), F32)
     share_of = LOSS_SCALE / weight_total
+    half_share = 0.5 * share_of
     p[2] = to_second(2, p[2])
     p[3] = to_second(3, p[3])
     xf = x_third(xf)
     xa = to_third(0, p)
     g = g_to_all(g, share_of)
     xb = to_third(1, p)
-    finish(0, xa, share_of)
+    finish(0, xa, half_share)
     g = g_to_sibling(g)
-    x_finish(xf, share_of)
+    x_finish(xf, half_share)
     g_finish(g)
-    finish(1, xb, share_of)
+    finish(1, xb, half_share)
     for left in leaving.values():
         left()
 

time: 48.4 us -> 48.5 us (level)
  no operation moved by 1% of the time
where the time goes in v7:
time: 48.5 us; the launch traced here: 48.4 us
  Pallas kernels  46.9 us (97%)
  between operations  1.45 us (3%)
    pallas_call x1, Pallas kernels, per_device(): pl.pallas_call(kernel, out_shape=[V((8, LANES), F32), V(latent.shape, BF1...  44.2 us
    pallas_call x1, Pallas kernels, per_device(): pl.pallas_call(write_out, out_shape=[jax.ShapeDtypeStruct((1, 1), F32), j...  2.68 us

profile of v7, /device:TPU:1, one launch (start us, length us, event | category | flops | bytes accessed | tf_op | source)
XLA Modules:
  0.0 48.4 jit_solution(7801787982059930272)
XLA Ops:
  1.3 44.2 %energy_step.1 = (f32[8,128]{1,0:T(8,128)S(1)}, bf16[2,1024,1024]{2,1,0:T(8,128)(2,1)S(1)}, f32[32,1024]{1,0:T(8,128)S(1)}, f32[80,1024]{1,0:T(8,128)S(1)}) custom-call(bf16[2,1024,1024]{2,1,0:T(8,128)(2,1)} %lat_hbm.1, bf16[1024,1024]{1,0:T(8,128)(2,1)} %w_hbm.1, bf16[80,1024]{1,0:T(8,128)(2,1)} %wout_hbm.1, bf16[80,1024]{1,0:T(8,128)(2,1)} %targets_hbm.1, ...), custom_call_target="tpu_custom_call" | custom-call | tf_op jit(solution)/shard_map/energy_step/pallas_call | solution.py:547
  45.5 2.7 %write_out.1 = (f32[1,1]{1,0:T(1,128)}, bf16[2,1024,1024]{2,1,0:T(8,128)(2,1)}, f32[32,1024]{1,0:T(8,128)}, f32[80,1024]{1,0:T(8,128)}) custom-call(f32[8,128]{1,0:T(8,128)S(1)} %get-tuple-element.12.loss, bf16[2,1024,1024]{2,1,0:T(8,128)(2,1)S(1)} %get-tuple-element.13.glat, f32[32,1024]{1,0:T(8,128)S(1)} %get-tuple-element.14.gwin, ...), custom_call_target="tpu_custom_call" | custom-call | tf_op jit(solution)/shard_map/write_out/pallas_call | solution.py:561
